TPU v7x, 256 devices: a whole 4x4x8 slice. The times are simulated.
256 devices in a mesh: row: 16 (over y_hi, x, core), col: 16 (over y_lo, z).
Axes of the slice: x: 4, y: 4 (y_hi: 2, y_lo: 2; y = y_hi * 2 + y_lo), z: 8, core: 2. Of those that a mesh axis runs over, the one named last changes fastest.
Arguments:
- basis_codes: bfloat16 [7168, 7168], P('row', 'col'), may hold values from -4 to 4
- code_scales: float32 [56, 7168], P(None, 'col'), may hold values from 0.006 to 0.06
- new_basis: float32 [7168, 7168], P('col', 'row'), may hold values from -6 to 6
- moment: float32 [7168, 9216], P('row', 'col'), may hold values from -0.0625 to 0.0625
Outputs:
- margin: float32 [7168, 7168], P('row', 'col')
- rotated_moment: float32 [7168, 9216], P('row', 'col')
All inputs are finite; a program needn't handle non-finite values.
Results may differ from a plain program's by a relative error of at most 0.0057.
Values may be sent and summed in bfloat16 or wider, within the bound.
No kernel may reach another device: no remote copies, remote signals or barrier semaphores. Data moves between devices by JAX's collectives and lax.ppermute only.
A program may use at most 128 MiB of HBM per device.

v0:
```python
import jax
import jax.numpy as jnp
from jax import lax
from jax.sharding import PartitionSpec as P


def body(basis_codes, code_scales, new_basis, moment):
    block_rows = basis_codes.shape[0]
    moment_rounded = moment.astype(jnp.bfloat16)
    scale_table = jnp.repeat(code_scales, 128, axis=0)
    factors = lax.dynamic_slice_in_dim(
        scale_table, lax.axis_index("row") * block_rows, basis_codes.shape[0], 0
    )
    own_old = (basis_codes.astype(jnp.float32) * factors).astype(jnp.bfloat16)
    old_panel = lax.all_gather(own_old, "row", axis=0, tiled=True)
    new_rounded = new_basis.astype(jnp.bfloat16)
    matched = old_panel
    margin = lax.dot_general(
        lax.all_gather(new_rounded, "col", axis=0, tiled=True),
        matched,
        (((0,), (0,)), ((), ())),
        preferred_element_type=jnp.float32,
    )
    margin_panel = lax.all_gather(margin.astype(jnp.bfloat16), "col", axis=1, tiled=True)
    matched = margin_panel
    rotated_moment = jnp.dot(
        matched,
        lax.all_gather(moment_rounded, "row", axis=0, tiled=True),
        preferred_element_type=jnp.float32,
    )
    return (margin, rotated_moment)


def solution(mesh):
    return jax.shard_map(
        body,
        mesh=mesh,
        in_specs=(P("row", "col"), P(None, "col"), P("col", "row"), P("row", "col")),
        out_specs=(P("row", "col"), P("row", "col")),
        check_vma=False,
    )
```

profile of v0, /device:TPU:8, one launch (start us, length us, event | category | flops | bytes accessed | tf_op | source)
XLA Modules:
  0.0 367.7 jit_solution(14049143547440517810)
XLA Ops:
  7.2 0.0 all-gather.5.cloned.1.call-start
  7.2 0.0 copy-start.2
  7.2 0.0 copy-start.1
  7.2 0.0 copy-start
  7.2 2.9 broadcast_in_dim.3
  10.2 0.0 copy-done.2
  10.2 0.9 multiply_convert_fusion
  11.1 0.0 all-gather.5.cloned.1.call-update
  11.1 0.0 all-gather.7.cloned.1.call-start
  11.2 0.0 copy-done.1
  11.2 0.8 convert_element_type.17
  12.0 0.0 all-gather.7.cloned.1.call-update
  12.0 0.0 all-gather.11.cloned.1.call-start
  12.1 0.0 copy-done
  12.1 0.9 convert_element_type.19
  13.0 0.0 all-gather.11.cloned.1.call-update
  13.0 0.0 all-gather.9.cloned.1.call-start
  13.0 74.0 %all-gather.5.cloned.1.call-done = bf16[7168,448]{1,0:T(8,128)(2,1)} async-done(((bf16[448,448]{1,0:T(8,128)(2,1)}), bf16[7168,448]{1,0:T(8,128)(2,1)}) %all-gather.5.cloned.1.call-update) | async-done | bytes 6422544 | tf_op jit(solution)/shard_map/all_gather | solution.py:15
  87.0 90.2 %all-gather.7.cloned.1.call-done = bf16[7168,448]{1,0:T(8,128)(2,1)} async-done(((bf16[448,448]{1,0:T(8,128)(2,1)}), bf16[7168,448]{1,0:T(8,128)(2,1)}) %all-gather.7.cloned.1.call-update) | async-done | bytes 6422544 | tf_op jit(solution)/shard_map/all_gather | solution.py:19
  177.2 9.4 %fusion = (bf16[448,448]{0,1:T(8,128)(2,1)}, f32[448,448]{0,1:T(8,128)S(1)}) fusion(bf16[7168,448]{1,0:T(8,128)(2,1)} %all-gather.5.cloned.1.call-done, bf16[7168,448]{1,0:T(8,128)(2,1)} %all-gather.7.cloned.1.call-done), kind=kOutput, calls=%fused_computation.2 | convolution fusion | flops 2877493248 | bytes 14049280 | tf_op jit(solution)/shard_map/dot_general | solution.py:18
  186.6 0.0 all-gather.9.cloned.1.call-update
  186.6 1.2 copy.6
  187.9 71.5 %all-gather.11.cloned.1.call-done = bf16[7168,576]{1,0:T(8,128)(2,1)} async-done(((bf16[448,576]{1,0:T(8,128)(2,1)}), bf16[7168,576]{1,0:T(8,128)(2,1)}) %all-gather.11.cloned.1.call-update) | async-done | bytes 8257552 | tf_op jit(solution)/shard_map/all_gather | solution.py:28
  259.3 90.0 %all-gather.9.cloned.1.call-done = bf16[448,7168]{0,1:T(8,128)(2,1)} async-done(((bf16[448,448]{0,1:T(8,128)(2,1)}), bf16[448,7168]{0,1:T(8,128)(2,1)}) %all-gather.9.cloned.1.call-update) | async-done | bytes 6422544 | tf_op jit(solution)/shard_map/all_gather | solution.py:24
  349.3 11.9 %fusion.1 = f32[448,576]{1,0:T(8,128)} fusion(bf16[448,7168]{0,1:T(8,128)(2,1)} %all-gather.9.cloned.1.call-done, bf16[7168,576]{1,0:T(8,128)(2,1)} %all-gather.11.cloned.1.call-done), kind=kOutput, calls=%fused_computation.3 | convolution fusion | flops 3699376128 | bytes 15712256 | tf_op jit(solution)/shard_map/dot_general | solution.py:26
Async XLA Ops:
  7.2 79.8 %all-gather.5.cloned.1.call-start = ((), (), s32[]{:S(2)}) async-start(), calls=%async_computation | async-start | bytes 7798784 | tf_op jit(solution)/shard_map/all_gather | solution.py:15
  7.2 3.0 copy-start.2
  7.2 3.9 %copy-start.1 = (f32[448,448]{1,0:T(8,128)S(1)}, f32[448,448]{1,0:T(8,128)}, u32[]{:S(2)}) copy-start(f32[448,448]{1,0:T(8,128)} %param.6) | copy-start | bytes 2408452
  7.2 4.8 %copy-start = (f32[448,576]{1,0:T(8,128)S(1)}, f32[448,576]{1,0:T(8,128)}, u32[]{:S(2)}) copy-start(f32[448,576]{1,0:T(8,128)} %param.7) | copy-start | bytes 3096580
  11.1 166.0 %all-gather.7.cloned.1.call-start = ((), (), s32[]{:S(2)}) async-start(), calls=%async_computation.1 | async-start | bytes 7798784 | tf_op jit(solution)/shard_map/all_gather | solution.py:19
  12.0 247.3 %all-gather.11.cloned.1.call-start = ((), (), s32[]{:S(2)}) async-start(), calls=%async_computation.3 | async-start | bytes 9748480 | tf_op jit(solution)/shard_map/all_gather | solution.py:28
  13.0 336.4 %all-gather.9.cloned.1.call-start = ((), (), s32[]{:S(2)}) async-start(), calls=%async_computation.2 | async-start | bytes 7798784 | tf_op jit(solution)/shard_map/all_gather | solution.py:24
Sparse Core Ops, SparseCore 0:
  11.3 75.6 all-gather.4
  88.8 88.3 all-gather.6
  180.5 78.8 all-gather.10
  261.0 88.3 all-gather.8
where the time goes:
time: 370 us; the launch traced here: 368 us
  waiting for transfers between devices  326 us (88%)
  matrix products  21.3 us (6%)
  between operations  13.8 us (4%)
  local copies, waits for them, and re-layouts  4.17 us (1%)
    all_gather x1, waiting for transfers between devices, body(): lax.all_gather(new_rounded, 'col', axis=0, tiled=True)  90.2 us
    all_gather x1, waiting for transfers between devices, body(): lax.all_gather(margin.astype(jnp.bfloat16), 'col', axis=1, tiled=True)  90 us
    all_gather x1, waiting for transfers between devices, body(): old_panel = lax.all_gather(own_old, 'row', axis=0, tiled=True)  74 us
    all_gather x1, waiting for transfers between devices, body(): lax.all_gather(moment_rounded, 'row', axis=0, tiled=True)  71.5 us
    dot_general x1, matrix products, body(): jnp.dot(matched, lax.all_gather(moment_rounded, 'row', axis=0, tiled=True...  11.9 us
    dot_general x1, matrix products, body(): lax.dot_general(lax.all_gather(new_rounded, 'col', axis=0, tiled=True), m...  9.43 us
  transfers between devices with their start and end apart: 4, of which 4 were waited for; matrix products, arithmetic and copies ran while one was open for 3% of the time, Pallas kernels for 0%

commit v1 on v0

v1 whole, which is shorter than its diff:
```python
import functools

import jax
import jax.numpy as jnp
from jax import lax
from jax.experimental import pallas as pl
from jax.experimental.pallas import tpu as pltpu
from jax.sharding import PartitionSpec as P

AXES = ("row", "col")
B = 448
HALF = B // 2
QUARTER = B // 4


def dev(x, yh, yl, z, c):
    return (yh * 8 + x * 2 + c) * 16 + yl * 8 + z


def everyone():
    return [
        (x, yh, yl, z, c)
        for x in range(4)
        for yh in range(2)
        for yl in range(2)
        for z in range(8)
        for c in range(2)
    ]


def perm_of(move):
    return [(dev(*d), dev(*move(*d))) for d in everyone()]


Z_UP = perm_of(lambda x, yh, yl, z, c: (x, yh, yl, (z + 1) % 8, c))
Z_DOWN = perm_of(lambda x, yh, yl, z, c: (x, yh, yl, (z - 1) % 8, c))
X_UP = perm_of(lambda x, yh, yl, z, c: ((x + 1) % 4, yh, yl, z, c))
X_DOWN = perm_of(lambda x, yh, yl, z, c: ((x - 1) % 4, yh, yl, z, c))
CORE = perm_of(lambda x, yh, yl, z, c: (x, yh, yl, z, 1 - c))
YL = perm_of(lambda x, yh, yl, z, c: (x, yh, 1 - yl, z, c))
Y_SWAP_TO = {0: 3, 3: 0, 1: 2, 2: 1}
Y_OUT_TO = {1: 0, 2: 3, 0: 1, 3: 2}


def y_perm(to, senders):
    def move(x, yh, yl, z, c):
        y = to[yh * 2 + yl]
        return (x, y // 2, y % 2, z, c)

    return [
        (dev(*d), dev(*move(*d))) for d in everyone() if d[1] * 2 + d[2] in senders
    ]


Y_SWAP = y_perm(Y_SWAP_TO, (0, 1, 2, 3))
Y_OUT = y_perm(Y_OUT_TO, (1, 2))
Y_RELAY = y_perm(Y_OUT_TO, (0, 3))


def send(v, perm):
    return lax.ppermute(v, AXES, perm)


def rounds(*values):
    return lax.optimization_barrier(values)


def call(kernel, shapes, operands, flops=0, space=pltpu.VMEM, scratch=(), grant=12):
    shapes = [jax.ShapeDtypeStruct(shape, kind) for shape, kind in shapes]
    moved = sum(v.size * v.dtype.itemsize for v in [*operands, *shapes])
    return pl.pallas_call(
        kernel,
        out_shape=shapes,
        in_specs=[pl.BlockSpec(memory_space=space)] * len(operands),
        out_specs=[pl.BlockSpec(memory_space=pltpu.VMEM)] * len(shapes),
        scratch_shapes=scratch,
        compiler_params=pltpu.CompilerParams(vmem_limit_bytes=grant * 1024 * 1024),
        cost_estimate=pl.CostEstimate(
            flops=flops, bytes_accessed=moved, transcendentals=0
        ),
    )(*operands)


def packed(v):
    n = v.shape[0] // 2
    return jnp.concatenate([v[:n], v[n:]], axis=1)


def unpacked(v):
    m = v.shape[1] // 2
    return jnp.concatenate([v[:, :m], v[:, m:]], axis=0)


def bases_kernel(new_hbm, codes_hbm, scales_hbm, new_out, old_out, new_ref, codes_ref, scales_ref, sems):
    copies = [
        pltpu.make_async_copy(source, target, sems.at[n])
        for n, (source, target) in enumerate(
            ((new_hbm, new_ref), (codes_hbm, codes_ref), (scales_hbm, scales_ref))
        )
    ]
    for copy in copies:
        copy.start()
    copies[0].wait()
    new_out[...] = packed(new_ref[...].T.astype(jnp.bfloat16))
    r = lax.axis_index("row")
    odd = lax.rem(r, 2) == 1
    first = lax.div(r * 7, 2)
    copies[1].wait()
    copies[2].wait()
    for k in range(7):
        rows = slice(k * 64, (k + 1) * 64)
        group = first + jnp.where(odd, (k + 1) // 2, k // 2)
        scale = scales_ref[pl.ds(group, 1), :]
        part = (codes_ref[rows].astype(jnp.float32) * scale).astype(jnp.bfloat16)
        if k < 3:
            old_out[rows, :B] = part
        elif k == 3:
            old_out[k * 64 :, :B] = part[:32]
            old_out[:32, B:] = part[32:]
        else:
            old_out[k * 64 - HALF : (k + 1) * 64 - HALF, B:] = part


OLD_ORDER = ((0, 0), (0, 1), (1, 0), (1, 1), (3, 0), (3, 1), (2, 0), (2, 1))


def margin_kernel(slot, a_ref, *refs):
    b_refs, outs, (a_buf, b_buf, sems) = refs[:8], refs[8:10], refs[10:]
    row = lax.axis_index("row")
    x = lax.div(lax.rem(row, 8), 2)
    c = lax.rem(row, 2)
    copies = []
    for n, (t, u) in enumerate(OLD_ORDER):
        kb = lax.rem(x + t, 4) * 2 + (c if u == 0 else 1 - c)
        copies.append(
            (
                pltpu.make_async_copy(a_ref.at[kb], a_buf.at[n], sems.at[0, n]),
                pltpu.make_async_copy(b_refs[n], b_buf.at[n], sems.at[1, n]),
            )
        )
    for pair in copies:
        for priority, copy in enumerate(pair):
            copy.start(priority=priority)
    total = None
    for n, pair in enumerate(copies):
        for copy in pair:
            copy.wait()
        term = jnp.dot(
            unpacked(a_buf[n]), unpacked(b_buf[n]), preferred_element_type=jnp.float32
        )
        total = term if total is None else total + term
    for half, out_ref in enumerate(outs):
        part = total[half * HALF : (half + 1) * HALF]
        out_ref[...] = packed(part.astype(jnp.bfloat16)) if slot == 0 else part


MARGIN_SCRATCH = (
    pltpu.VMEM((8, HALF, 2 * B), jnp.bfloat16),
    pltpu.VMEM((8, HALF, 2 * B), jnp.bfloat16),
    pltpu.SemaphoreType.DMA((2, 8)),
)


def margin_sum_kernel(keep_ref, other_ref, margin_ref, out_ref):
    margin = keep_ref[...] + unpacked(other_ref[...]).astype(jnp.float32)
    margin_ref[...] = margin
    out_ref[...] = packed(margin.astype(jnp.bfloat16))


def moment_kernel(moment_ref, out_ref):
    out_ref[...] = packed(moment_ref[...].astype(jnp.bfloat16))


def moment_pair_kernel(own_ref, in_ref, out_ref, relay_ref, pair_ref):
    edge = lax.div(lax.axis_index("col"), 8) == lax.div(lax.axis_index("row"), 8)
    width = pair_ref.shape[1] // 2

    @pl.when(edge)
    def _():
        pair_ref[:, :width] = unpacked(out_ref[...])
        pair_ref[:, width:] = unpacked(own_ref[...])

    @pl.when(jnp.logical_not(edge))
    def _():
        pair_ref[:, :width] = unpacked(in_ref[...])
        pair_ref[:, width:] = unpacked(relay_ref[...])


def rotate_kernel(slot, b_ref, *refs):
    a_refs, out_ref = refs[:8], refs[8]
    z = lax.rem(lax.axis_index("col"), 8)
    width = b_ref.shape[2] // 2
    total = None
    for s in range(8):
        term = jnp.dot(
            unpacked(a_refs[s][...]),
            b_ref[lax.rem(z + s, 8), :, slot * width : (slot + 1) * width],
            preferred_element_type=jnp.float32,
        )
        total = term if total is None else total + term
    out_ref[...] = packed(total.astype(jnp.bfloat16)) if slot == 0 else total


def rotate_sum_kernel(keep_a, other_a, keep_b, other_b, out_ref):
    out_ref[:HALF] = keep_a[...] + unpacked(other_a[...]).astype(jnp.float32)
    out_ref[HALF:] = keep_b[...] + unpacked(other_b[...]).astype(jnp.float32)


def z_gather(top, bottom, margin):
    rings = []
    ups, downs = ([top], [bottom]), ([top], [bottom])
    for step in range(4):
        for i in range(2):
            if step < 3 or i == 0:
                ups[i].append(send(ups[i][-1], Z_UP))
            if step < 3 or i == 1:
                downs[i].append(send(downs[i][-1], Z_DOWN))
        if step == 1:
            ups[0][-1], margin = rounds(ups[0][-1], margin)
    for i in range(2):
        u, d = ups[i], downs[i]
        far = u[4] if i == 0 else d[4]
        rings.append([u[0], d[1], d[2], d[3], far, u[3], u[2], u[1]])
    return rings, margin


def body(basis_codes, code_scales, new_basis, moment):
    width = moment.shape[1]
    bf16, f32 = jnp.bfloat16, jnp.float32
    new_t, o = call(
        bases_kernel,
        [((HALF, 2 * B), bf16)] * 2,
        [new_basis, basis_codes, code_scales],
        space=pl.ANY,
        scratch=(
            pltpu.VMEM((B, B), f32),
            pltpu.VMEM((B, B), bf16),
            pltpu.VMEM(code_scales.shape, f32),
            pltpu.SemaphoreType.DMA((3,)),
        ),
        grant=60,
    )
    groups8 = [list(range(8)), list(range(8, 16))]
    a_all = lax.all_gather(new_t, "col", axis_index_groups=groups8)
    edge = lax.axis_index("col") // 8 == lax.axis_index("row") // 8

    o_in, o_out = send(o, Y_SWAP), send(o, Y_OUT)
    o_in, o_out, moment = rounds(o_in, o_out, moment)
    o0 = jnp.where(edge, o_out, o_in)
    o_relay, o0b, o0a = send(o_in, Y_RELAY), send(o0, X_UP), send(o0, X_DOWN)
    (m,) = call(moment_kernel, [((HALF, 2 * width), bf16)], [moment])
    m_in, m_out = send(m, Y_SWAP), send(m, Y_OUT)
    o_relay, o0b, o0a = rounds(o_relay, o0b, o0a)
    o1 = jnp.where(edge, o, o_relay)
    o1b, o1a = send(o1, X_UP), send(o1, X_DOWN)
    m_in, o0a_, o0b_ = rounds(m_in, o0a, o0b)
    m_out, o0a_, o0b_ = rounds(m_out, o0a_, o0b_)
    o0ac, o0bc, m_relay = send(o0a_, CORE), send(o0b_, CORE), send(m_in, Y_RELAY)
    o1b, o1a, o0b, o0, o0ac, o0bc = rounds(o1b, o1a, o0b, o0, o0ac, o0bc)
    o0f, o1f = send(o0b, X_UP), send(o1a, X_DOWN)
    o0c = send(o0, CORE)
    (m01,) = call(moment_pair_kernel, [((B, 2 * width), bf16)], [m, m_in, m_out, m_relay])
    o0f, o1f, o0c, m01 = rounds(o0f, o1f, o0c, m01)
    m_all = lax.all_gather(m01, "row", axis_index_groups=groups8)
    o0f, o1f, a_all = rounds(o0f, o1f, a_all)
    o0fc, o1fc = send(o0f, CORE), send(o1f, CORE)
    o0fc, *near_1 = rounds(o0fc, o1, o1a, o1b)
    o1c, o1ac, o1bc = (send(v, CORE) for v in near_1)

    others = call(
        functools.partial(margin_kernel, 0),
        [((QUARTER, 2 * B), bf16)] * 2,
        [a_all, o0, o0c, o0a, o0ac, o0b, o0bc, o0f, o0fc],
        flops=2 * B * B * 8 * B,
        space=pl.ANY,
        scratch=MARGIN_SCRATCH,
        grant=58,
    )
    keeps = call(
        functools.partial(margin_kernel, 1),
        [((HALF, B), f32)] * 2,
        [a_all, o1, o1c, o1a, o1ac, o1b, o1bc, o1f, o1fc],
        flops=2 * B * B * 8 * B,
        space=pl.ANY,
        scratch=MARGIN_SCRATCH,
        grant=58,
    )
    margins, halves = [], []
    for keep, other in zip(keeps, others):
        margin, half = call(
            margin_sum_kernel,
            [((HALF, B), f32), ((QUARTER, 2 * B), bf16)],
            [keep, send(other, YL)],
        )
        margins.append(margin)
        halves.append(half)
    margin = jnp.stack(margins).reshape(B, B)
    rings, margin = z_gather(*halves, margin)
    parts = []
    for slot in range(2):
        for half, ring in enumerate(rings):
            shape = ((QUARTER, 2 * width), bf16) if slot == 0 else ((HALF, width), f32)
            (out,) = call(
                functools.partial(rotate_kernel, slot),
                [shape],
                [m_all, *ring],
                flops=2 * HALF * B * 8 * width,
            )
            parts.append(send(out, YL) if slot == 0 else out)
    other_a, other_b, keep_a, keep_b = parts
    (rotated,) = call(
        rotate_sum_kernel, [((B, width), f32)], [keep_a, other_a, keep_b, other_b]
    )
    return margin, rotated


def solution(mesh):
    return jax.shard_map(
        body,
        mesh=mesh,
        in_specs=(P("row", "col"), P(None, "col"), P("col", "row"), P("row", "col")),
        out_specs=(P("row", "col"), P("row", "col")),
        check_vma=False,
    )
```

time: 370 us -> 142 us (0.38)
  waiting for transfers between devices: 326 us -> 40.3 us
  starting transfers between devices: 0.16 us -> 53.3 us
  Pallas kernels: 0 us -> 24.5 us
  matrix products: 21.3 us -> 0 us
  local copies, waits for them, and re-layouts: 4.17 us -> 7.95 us
    all_gather x4 -> x2, waiting for transfers between devices: 326 us -> 0.02 us  [the longest x1 0.02 us: body(): a_all = lax.all_gather(new_t, 'col', axis_index_groups=groups8)]
    ppermute x0 -> x38, starting transfers between devices: none -> 53.2 us  [send(): return lax.ppermute(v, AXES, perm)]
    ppermute x0 -> x38, waiting for transfers between devices: none -> 40.2 us  [send(): return lax.ppermute(v, AXES, perm)]
    pallas_call x0 -> x12, Pallas kernels: none -> 24.5 us  [call(): pl.pallas_call(kernel, out_shape=shapes, in_specs=[pl.BlockSpec(memory_sp...]
    dot_general x2 -> x0, matrix products: 21.3 us -> none  [the longest x1 11.9 us: body(): jnp.dot(matched, lax.all_gather(moment_rounded, 'row', axis=0, tiled=True...]
    unnamed x7 -> x38, local copies, waits for them, and re-layouts: 1.26 us -> 7.95 us
  transfers between devices with their start and end apart: 4 -> 40, of which waited for: 4 -> 17; matrix products, arithmetic and copies ran while one was open for 3% -> 1% of each run, Pallas kernels for 0% -> 15%
where the time goes in v1:
time: 142 us
  starting transfers between devices  53.3 us (38%)
  waiting for transfers between devices  40.3 us (28%)
  Pallas kernels  24.5 us (17%)
  between operations  14.4 us (10%)
  local copies, waits for them, and re-layouts  7.95 us (6%)
    ppermute x38, starting transfers between devices, send(): return lax.ppermute(v, AXES, perm)  53.2 us
    ppermute x38, waiting for transfers between devices, send(): return lax.ppermute(v, AXES, perm)  40.2 us
    pallas_call x12, Pallas kernels, call(): pl.pallas_call(kernel, out_shape=shapes, in_specs=[pl.BlockSpec(memory_sp...  24.5 us
    unnamed x38, local copies, waits for them, and re-layouts  7.95 us
  transfers between devices with their start and end apart: 40, of which 17 were waited for; matrix products, arithmetic and copies ran while one was open for 1% of the time, Pallas kernels for 15%

profile of v1, /device:TPU:8, one launch (start us, length us, event | category | flops | bytes accessed | tf_op | source)
XLA Modules:
  0.0 141.5 jit_solution(2914097336352893120)
XLA Ops:
  7.2 2.6 %shard_map.59 = (bf16[224,896]{1,0:T(8,128)(2,1)}, bf16[224,896]{1,0:T(8,128)(2,1)}) custom-call(f32[448,448]{1,0:T(8,128)} %new_hbm.1, bf16[448,448]{1,0:T(8,128)(2,1)} %codes_hbm.1, f32[56,448]{1,0:T(8,128)} %scales_hbm.1), custom_call_target="tpu_custom_call" | custom-call | bytes 2107392 | tf_op jit(solution)/shard_map/pallas_call | solution.py:71
  9.9 1.7 %collective-permute-start = (bf16[224,896]{1,0:T(8,128)(2,1)}, bf16[224,896]{1,0:T(8,128)(2,1)S(1)}, u32[]{:S(2)}, u32[]{:S(2)}) collective-permute-start(bf16[224,896]{1,0:T(8,128)(2,1)} %get-tuple-element.43), channel_id=1, source_target_pairs={{0,136},{16,152},{1,137},{17,153},{2,138},{18,154},{3,139},{19,155... | collective-permute-start | bytes 1204232 | tf_op jit(solution)/shard_map/ppermute | solution.py:61
  11.5 3.8 %collective-permute-start.1 = (bf16[224,896]{1,0:T(8,128)(2,1)}, bf16[224,896]{1,0:T(8,128)(2,1)S(1)}, u32[]{:S(2)}, u32[]{:S(2)}) collective-permute-start(bf16[224,896]{1,0:T(8,128)(2,1)} %get-tuple-element.43), channel_id=1, source_target_pairs={{8,0},{24,16},{9,1},{25,17},{10,2},{26,18},{11,3},{27,19},{12,4},{... | collective-permute-start | bytes 1204232 | tf_op jit(solution)/shard_map/ppermute | solution.py:61
  15.4 5.8 %collective-permute-done = bf16[224,896]{1,0:T(8,128)(2,1)S(1)} collective-permute-done((bf16[224,896]{1,0:T(8,128)(2,1)}, bf16[224,896]{1,0:T(8,128)(2,1)S(1)}, u32[]{:S(2)}, u32[]{:S(2)}) %collective-permute-start) | collective-permute-done | bytes 401440 | tf_op jit(solution)/shard_map/ppermute | solution.py:61
  21.2 2.7 %collective-permute-done.1 = bf16[224,896]{1,0:T(8,128)(2,1)S(1)} collective-permute-done((bf16[224,896]{1,0:T(8,128)(2,1)}, bf16[224,896]{1,0:T(8,128)(2,1)S(1)}, u32[]{:S(2)}, u32[]{:S(2)}) %collective-permute-start.1) | collective-permute-done | bytes 401440 | tf_op jit(solution)/shard_map/ppermute | solution.py:61
  26.8 1.7 %collective-permute-start.4 = (bf16[224,896]{1,0:T(8,128)(2,1)S(1)}, bf16[224,896]{1,0:T(8,128)(2,1)S(1)}, u32[]{:S(2)}, u32[]{:S(2)}) collective-permute-start(bf16[224,896]{1,0:T(8,128)(2,1)S(1)} %broadcast_select_fusion.1.refs_0_), channel_id=1, source_target_pairs={{0,96},{16,112},{1,97},{17,113},{2,98},{18,114},{3,99},{19,115},{4... | collective-permute-start | bytes 1204232 | tf_op jit(solution)/shard_map/ppermute | solution.py:61
  28.8 4.9 %collective-permute-start.7 = (bf16[224,1152]{1,0:T(8,128)(2,1)S(1)}, bf16[224,1152]{1,0:T(8,128)(2,1)S(1)}, u32[]{:S(2)}, u32[]{:S(2)}) collective-permute-start(bf16[224,1152]{1,0:T(8,128)(2,1)S(1)} %shard_map.60.own_ref), channel_id=1, source_target_pairs={{8,0},{24,16},{9,1},{25,17},{10,2},{26,18},{11,3},{27,19},{12,4},{... | collective-permute-start | bytes 1548296 | tf_op jit(solution)/shard_map/ppermute | solution.py:61
  33.7 1.9 %collective-permute-done.2 = bf16[224,896]{1,0:T(8,128)(2,1)S(1)} collective-permute-done((bf16[224,896]{1,0:T(8,128)(2,1)S(1)}, bf16[224,896]{1,0:T(8,128)(2,1)S(1)}, u32[]{:S(2)}, u32[]{:S(2)}) %collective-permute-start.2) | collective-permute-done | bytes 401440 | tf_op jit(solution)/shard_map/ppermute | solution.py:61
  38.0 1.8 %collective-permute-start.6 = (bf16[224,896]{1,0:T(8,128)(2,1)S(1)}, bf16[224,896]{1,0:T(8,128)(2,1)S(1)}, u32[]{:S(2)}, u32[]{:S(2)}) collective-permute-start(bf16[224,896]{1,0:T(8,128)(2,1)S(1)} %broadcast_select_fusion.refs_0_), channel_id=1, source_target_pairs={{0,96},{16,112},{1,97},{17,113},{2,98},{18,114},{3,99},{19,115},{4... | collective-permute-start | bytes 1204232 | tf_op jit(solution)/shard_map/ppermute | solution.py:61
  40.5 1.8 %collective-permute-done.7.out_ref = bf16[224,1152]{1,0:T(8,128)(2,1)S(1)} collective-permute-done((bf16[224,1152]{1,0:T(8,128)(2,1)S(1)}, bf16[224,1152]{1,0:T(8,128)(2,1)S(1)}, u32[]{:S(2)}, u32[]{:S(2)}) %collective-permute-start.7) | collective-permute-done | bytes 516128 | tf_op jit(solution)/shard_map/ppermute | solution.py:61
  44.2 2.6 %collective-permute-done.5.refs_4_ = bf16[224,896]{1,0:T(8,128)(2,1)S(1)} collective-permute-done((bf16[224,896]{1,0:T(8,128)(2,1)S(1)}, bf16[224,896]{1,0:T(8,128)(2,1)S(1)}, u32[]{:S(2)}, u32[]{:S(2)}) %collective-permute-start.5) | collective-permute-done | bytes 401440 | tf_op jit(solution)/shard_map/ppermute | solution.py:61
  48.5 2.4 %collective-permute-start.12 = (bf16[224,896]{1,0:T(8,128)(2,1)S(1)}, bf16[224,896]{1,0:T(8,128)(2,1)S(1)}, u32[]{:S(2)}, u32[]{:S(2)}) collective-permute-start(bf16[224,896]{1,0:T(8,128)(2,1)S(1)} %collective-permute-done.6.refs_2_), channel_id=1, source_target_pairs={{0,96},{16,112},{1,97},{17,113},{2,98},{18,114},{3,99},{19,115},{4... | collective-permute-start | bytes 1204232 | tf_op jit(solution)/shard_map/ppermute | solution.py:61
  50.9 7.7 %collective-permute-done.14.relay_ref = bf16[224,1152]{1,0:T(8,128)(2,1)S(1)} collective-permute-done((bf16[224,1152]{1,0:T(8,128)(2,1)S(1)}, bf16[224,1152]{1,0:T(8,128)(2,1)S(1)}, u32[]{:S(2)}, u32[]{:S(2)}) %collective-permute-start.14) | collective-permute-done | bytes 516128 | tf_op jit(solution)/shard_map/ppermute | solution.py:61
  62.8 5.8 %shard_map.63 = (bf16[112,896]{1,0:T(8,128)(2,1)}, bf16[112,896]{1,0:T(8,128)(2,1)}) custom-call(bf16[8,224,896]{2,1,0:T(8,128)(2,1)} %bitcast.11, bf16[224,896]{1,0:T(8,128)(2,1)} %copy-done.5, bf16[224,896]{1,0:T(8,128)(2,1)} %collective-permute-done.13.refs_1_, bf16[224,896]{1,0:T(8,128)(2,1)} %copy-done.9, bf16[224,896]{1,0:T(8,128)(2,1)} %copy-done.11, ...), custom_call_target="tpu_custom_call" | custom-call | flops 1438646272 | bytes 6823936 | tf_op jit(solution)/shard_map/pallas_call | solution.py:71
  72.4 6.1 %shard_map.62 = (f32[224,448]{1,0:T(8,128)}, f32[224,448]{1,0:T(8,128)}) custom-call(bf16[8,224,896]{2,1,0:T(8,128)(2,1)} %bitcast.12, bf16[224,896]{1,0:T(8,128)(2,1)} %copy-done.4, bf16[224,896]{1,0:T(8,128)(2,1)} %copy-done.14, bf16[224,896]{1,0:T(8,128)(2,1)} %copy-done.8, bf16[224,896]{1,0:T(8,128)(2,1)} %copy-done.15, bf16[224,896]{1,0:T(8,128)(2,1)} %copy-done.6, ...), custom_call_target="tpu_custom_call" | custom-call | flops 1438646272 | bytes 7225344 | tf_op jit(solution)/shard_map/pallas_call | solution.py:71
  79.7 2.2 %collective-permute-start.21 = (bf16[112,896]{1,0:T(8,128)(2,1)S(1)}, bf16[112,896]{1,0:T(8,128)(2,1)S(1)}, u32[]{:S(2)}, u32[]{:S(2)}) collective-permute-start(bf16[112,896]{1,0:T(8,128)(2,1)S(1)} %get-tuple-element.75.refs_0_), channel_id=1, source_target_pairs={{0,1},{16,17},{1,2},{17,18},{2,3},{18,19},{3,4},{19,20},{4,5},{20,... | collective-permute-start | bytes 602120 | tf_op jit(solution)/shard_map/ppermute | solution.py:61
  83.1 4.6 %collective-permute-start.30 = (bf16[112,896]{1,0:T(8,128)(2,1)S(1)}, bf16[112,896]{1,0:T(8,128)(2,1)S(1)}, u32[]{:S(2)}, u32[]{:S(2)}) collective-permute-start(bf16[112,896]{1,0:T(8,128)(2,1)S(1)} %get-tuple-element.83.refs_0_), channel_id=1, source_target_pairs={{0,7},{16,23},{1,0},{17,16},{2,1},{18,17},{3,2},{19,18},{4,3},{20,... | collective-permute-start | bytes 602120 | tf_op jit(solution)/shard_map/ppermute | solution.py:61
  90.9 2.2 %collective-permute-done.30.refs_1_ = bf16[112,896]{1,0:T(8,128)(2,1)S(1)} collective-permute-done((bf16[112,896]{1,0:T(8,128)(2,1)S(1)}, bf16[112,896]{1,0:T(8,128)(2,1)S(1)}, u32[]{:S(2)}, u32[]{:S(2)}) %collective-permute-start.30) | collective-permute-done | bytes 200736 | tf_op jit(solution)/shard_map/ppermute | solution.py:61
  93.1 3.7 %collective-permute-start.31 = (bf16[112,896]{1,0:T(8,128)(2,1)S(1)}, bf16[112,896]{1,0:T(8,128)(2,1)S(1)}, u32[]{:S(2)}, u32[]{:S(2)}) collective-permute-start(bf16[112,896]{1,0:T(8,128)(2,1)S(1)} %collective-permute-done.30.refs_1_), channel_id=1, source_target_pairs={{0,7},{16,23},{1,0},{17,16},{2,1},{18,17},{3,2},{19,18},{4,3},{20,... | collective-permute-start | bytes 602120 | tf_op jit(solution)/shard_map/ppermute | solution.py:61
  97.8 3.3 %collective-permute-start.25 = (bf16[112,896]{1,0:T(8,128)(2,1)S(1)}, bf16[112,896]{1,0:T(8,128)(2,1)S(1)}, u32[]{:S(2)}, u32[]{:S(2)}) collective-permute-start(bf16[112,896]{1,0:T(8,128)(2,1)S(1)} %collective-permute-done.24.refs_1_), channel_id=1, source_target_pairs={{0,7},{16,23},{1,0},{17,16},{2,1},{18,17},{3,2},{19,18},{4,3},{20,... | collective-permute-start | bytes 602120 | tf_op jit(solution)/shard_map/ppermute | solution.py:61
  101.1 1.9 %collective-permute-done.34.refs_7_ = bf16[112,896]{1,0:T(8,128)(2,1)S(1)} collective-permute-done((bf16[112,896]{1,0:T(8,128)(2,1)S(1)}, bf16[112,896]{1,0:T(8,128)(2,1)S(1)}, u32[]{:S(2)}, u32[]{:S(2)}) %collective-permute-start.34) | collective-permute-done | bytes 200736 | tf_op jit(solution)/shard_map/ppermute | solution.py:61
  103.0 3.2 %collective-permute-start.32 = (bf16[112,896]{1,0:T(8,128)(2,1)S(1)}, bf16[112,896]{1,0:T(8,128)(2,1)S(1)}, u32[]{:S(2)}, u32[]{:S(2)}) collective-permute-start(bf16[112,896]{1,0:T(8,128)(2,1)S(1)} %collective-permute-done.31.refs_2_), channel_id=1, source_target_pairs={{0,7},{16,23},{1,0},{17,16},{2,1},{18,17},{3,2},{19,18},{4,3},{20,... | collective-permute-start | bytes 602120 | tf_op jit(solution)/shard_map/ppermute | solution.py:61
  106.3 2.4 %collective-permute-start.26 = (bf16[112,896]{1,0:T(8,128)(2,1)S(1)}, bf16[112,896]{1,0:T(8,128)(2,1)S(1)}, u32[]{:S(2)}, u32[]{:S(2)}) collective-permute-start(bf16[112,896]{1,0:T(8,128)(2,1)S(1)} %collective-permute-done.25.refs_2_), channel_id=1, source_target_pairs={{0,7},{16,23},{1,0},{17,16},{2,1},{18,17},{3,2},{19,18},{4,3},{20,... | collective-permute-start | bytes 602120 | tf_op jit(solution)/shard_map/ppermute | solution.py:61
  109.1 3.3 %collective-permute-done.35.refs_6_ = bf16[112,896]{1,0:T(8,128)(2,1)S(1)} collective-permute-done((bf16[112,896]{1,0:T(8,128)(2,1)S(1)}, bf16[112,896]{1,0:T(8,128)(2,1)S(1)}, u32[]{:S(2)}, u32[]{:S(2)}) %collective-permute-start.35) | collective-permute-done | bytes 200736 | tf_op jit(solution)/shard_map/ppermute | solution.py:61
  112.4 3.2 %collective-permute-start.33 = (bf16[112,896]{1,0:T(8,128)(2,1)S(1)}, bf16[112,896]{1,0:T(8,128)(2,1)S(1)}, u32[]{:S(2)}, u32[]{:S(2)}) collective-permute-start(bf16[112,896]{1,0:T(8,128)(2,1)S(1)} %collective-permute-done.32.refs_3_), channel_id=1, source_target_pairs={{0,7},{16,23},{1,0},{17,16},{2,1},{18,17},{3,2},{19,18},{4,3},{20,... | collective-permute-start | bytes 602120 | tf_op jit(solution)/shard_map/ppermute | solution.py:61
  115.7 2.1 %collective-permute-done.28.refs_4_ = bf16[112,896]{1,0:T(8,128)(2,1)S(1)} collective-permute-done((bf16[112,896]{1,0:T(8,128)(2,1)S(1)}, bf16[112,896]{1,0:T(8,128)(2,1)S(1)}, u32[]{:S(2)}, u32[]{:S(2)}) %collective-permute-start.28) | collective-permute-done | bytes 200736 | tf_op jit(solution)/shard_map/ppermute | solution.py:61
  117.7 3.3 %copy-done = bf16[3584,1152]{1,0:T(8,128)(2,1)S(1)} copy-done((bf16[3584,1152]{1,0:T(8,128)(2,1)S(1)}, bf16[3584,1152]{1,0:T(8,128)(2,1)}, u32[]{:S(2)}) %copy-start) | copy-done | bytes 8257560
  121.1 1.7 %shard_map.67 = bf16[112,1152]{1,0:T(8,128)(2,1)S(1)} custom-call(bf16[8,448,1152]{2,1,0:T(8,128)(2,1)S(1)} %bitcast.5, bf16[112,896]{1,0:T(8,128)(2,1)S(1)} %get-tuple-element.75.refs_0_, bf16[112,896]{1,0:T(8,128)(2,1)S(1)} %collective-permute-done.24.refs_1_, bf16[112,896]{1,0:T(8,128)(2,1)S(1)} %collective-permute-done.25.refs_2_, ...), custom_call_target="tpu_custom_call" | custom-call | flops 924844032 | bytes 10121216 | tf_op jit(solution)/shard_map/pallas_call | solution.py:71
  123.3 1.7 %shard_map.69 = bf16[112,1152]{1,0:T(8,128)(2,1)S(1)} custom-call(bf16[8,448,1152]{2,1,0:T(8,128)(2,1)S(1)} %bitcast.6, bf16[112,896]{1,0:T(8,128)(2,1)S(1)} %get-tuple-element.83.refs_0_, bf16[112,896]{1,0:T(8,128)(2,1)S(1)} %collective-permute-done.30.refs_1_, bf16[112,896]{1,0:T(8,128)(2,1)S(1)} %collective-permute-done.31.refs_2_, ...), custom_call_target="tpu_custom_call" | custom-call | flops 924844032 | bytes 10121216 | tf_op jit(solution)/shard_map/pallas_call | solution.py:71
  126.7 1.8 %shard_map.66.keep_a = f32[224,576]{1,0:T(8,128)S(1)} custom-call(bf16[8,448,1152]{2,1,0:T(8,128)(2,1)S(1)} %bitcast.7, bf16[112,896]{1,0:T(8,128)(2,1)S(1)} %get-tuple-element.75.refs_0_, bf16[112,896]{1,0:T(8,128)(2,1)S(1)} %collective-permute-done.24.refs_1_, bf16[112,896]{1,0:T(8,128)(2,1)S(1)} %collective-permute-done.25.refs_2_, ...), custom_call_target="tpu_custom_call" | custom-call | flops 924844032 | bytes 10379264 | tf_op jit(solution)/shard_map/pallas_call | solution.py:71
  128.5 1.8 %shard_map.68.keep_b = f32[224,576]{1,0:T(8,128)S(1)} custom-call(bf16[8,448,1152]{2,1,0:T(8,128)(2,1)S(1)} %bitcast.8, bf16[112,896]{1,0:T(8,128)(2,1)S(1)} %get-tuple-element.83.refs_0_, bf16[112,896]{1,0:T(8,128)(2,1)S(1)} %collective-permute-done.30.refs_1_, bf16[112,896]{1,0:T(8,128)(2,1)S(1)} %collective-permute-done.31.refs_2_, ...), custom_call_target="tpu_custom_call" | custom-call | flops 924844032 | bytes 10379264 | tf_op jit(solution)/shard_map/pallas_call | solution.py:71
  130.7 2.8 %collective-permute-done.37.other_b = bf16[112,1152]{1,0:T(8,128)(2,1)S(1)} collective-permute-done((bf16[112,1152]{1,0:T(8,128)(2,1)S(1)}, bf16[112,1152]{1,0:T(8,128)(2,1)S(1)}, u32[]{:S(2)}, u32[]{:S(2)}) %collective-permute-start.37) | collective-permute-done | bytes 258080 | tf_op jit(solution)/shard_map/ppermute | solution.py:61
  (103 shorter events, 28.6 us)
Async XLA Ops:
  7.2 52.8 %all-gather.5.cloned.1.call-start = ((), (), s32[]{:S(2)}) async-start(), calls=%async_computation | async-start | bytes 3612672 | tf_op jit(solution)/shard_map/all_gather | solution.py:244
  9.8 107.9 %all-gather.7.cloned.1.call-start = ((), (), s32[]{:S(2)}) async-start(), calls=%async_computation.1 | async-start | bytes 9289728 | tf_op jit(solution)/shard_map/all_gather | solution.py:264
  9.9 11.3 %collective-permute-start = (bf16[224,896]{1,0:T(8,128)(2,1)}, bf16[224,896]{1,0:T(8,128)(2,1)S(1)}, u32[]{:S(2)}, u32[]{:S(2)}) collective-permute-start(bf16[224,896]{1,0:T(8,128)(2,1)} %get-tuple-element.43), channel_id=1, source_target_pairs={{0,136},{16,152},{1,137},{17,153},{2,138},{18,154},{3,139},{19,155... | collective-permute-start | bytes 1204232 | tf_op jit(solution)/shard_map/ppermute | solution.py:61
  11.5 12.4 %collective-permute-start.1 = (bf16[224,896]{1,0:T(8,128)(2,1)}, bf16[224,896]{1,0:T(8,128)(2,1)S(1)}, u32[]{:S(2)}, u32[]{:S(2)}) collective-permute-start(bf16[224,896]{1,0:T(8,128)(2,1)} %get-tuple-element.43), channel_id=1, source_target_pairs={{8,0},{24,16},{9,1},{25,17},{10,2},{26,18},{11,3},{27,19},{12,4},{... | collective-permute-start | bytes 1204232 | tf_op jit(solution)/shard_map/ppermute | solution.py:61
  23.9 11.7 %collective-permute-start.2 = (bf16[224,896]{1,0:T(8,128)(2,1)S(1)}, bf16[224,896]{1,0:T(8,128)(2,1)S(1)}, u32[]{:S(2)}, u32[]{:S(2)}) collective-permute-start(bf16[224,896]{1,0:T(8,128)(2,1)S(1)} %collective-permute-done), channel_id=1, source_target_pairs={{0,8},{16,24},{1,9},{17,25},{2,10},{18,26},{3,11},{19,27},{4,12},{... | collective-permute-start | bytes 1204232 | tf_op jit(solution)/shard_map/ppermute | solution.py:61
  25.3 11.1 %collective-permute-start.3 = (bf16[224,896]{1,0:T(8,128)(2,1)S(1)}, bf16[224,896]{1,0:T(8,128)(2,1)S(1)}, u32[]{:S(2)}, u32[]{:S(2)}) collective-permute-start(bf16[224,896]{1,0:T(8,128)(2,1)S(1)} %broadcast_select_fusion.1.refs_0_), channel_id=1, source_target_pairs={{0,32},{16,48},{1,33},{17,49},{2,34},{18,50},{3,35},{19,51},{4,36}... | collective-permute-start | bytes 1204232 | tf_op jit(solution)/shard_map/ppermute | solution.py:61
  26.8 9.6 %collective-permute-start.4 = (bf16[224,896]{1,0:T(8,128)(2,1)S(1)}, bf16[224,896]{1,0:T(8,128)(2,1)S(1)}, u32[]{:S(2)}, u32[]{:S(2)}) collective-permute-start(bf16[224,896]{1,0:T(8,128)(2,1)S(1)} %broadcast_select_fusion.1.refs_0_), channel_id=1, source_target_pairs={{0,96},{16,112},{1,97},{17,113},{2,98},{18,114},{3,99},{19,115},{4... | collective-permute-start | bytes 1204232 | tf_op jit(solution)/shard_map/ppermute | solution.py:61
  28.7 11.8 %collective-permute-start.8 = (bf16[224,1152]{1,0:T(8,128)(2,1)S(1)}, bf16[224,1152]{1,0:T(8,128)(2,1)S(1)}, u32[]{:S(2)}, u32[]{:S(2)}) collective-permute-start(bf16[224,1152]{1,0:T(8,128)(2,1)S(1)} %shard_map.60.own_ref), channel_id=1, source_target_pairs={{0,136},{16,152},{1,137},{17,153},{2,138},{18,154},{3,139},{19,155... | collective-permute-start | bytes 1548296 | tf_op jit(solution)/shard_map/ppermute | solution.py:61
  28.8 13.6 %collective-permute-start.7 = (bf16[224,1152]{1,0:T(8,128)(2,1)S(1)}, bf16[224,1152]{1,0:T(8,128)(2,1)S(1)}, u32[]{:S(2)}, u32[]{:S(2)}) collective-permute-start(bf16[224,1152]{1,0:T(8,128)(2,1)S(1)} %shard_map.60.own_ref), channel_id=1, source_target_pairs={{8,0},{24,16},{9,1},{25,17},{10,2},{26,18},{11,3},{27,19},{12,4},{... | collective-permute-start | bytes 1548296 | tf_op jit(solution)/shard_map/ppermute | solution.py:61
  36.5 10.3 %collective-permute-start.5 = (bf16[224,896]{1,0:T(8,128)(2,1)S(1)}, bf16[224,896]{1,0:T(8,128)(2,1)S(1)}, u32[]{:S(2)}, u32[]{:S(2)}) collective-permute-start(bf16[224,896]{1,0:T(8,128)(2,1)S(1)} %broadcast_select_fusion.refs_0_), channel_id=1, source_target_pairs={{0,32},{16,48},{1,33},{17,49},{2,34},{18,50},{3,35},{19,51},{4,36}... | collective-permute-start | bytes 1204232 | tf_op jit(solution)/shard_map/ppermute | solution.py:61
  38.0 8.8 %collective-permute-start.6 = (bf16[224,896]{1,0:T(8,128)(2,1)S(1)}, bf16[224,896]{1,0:T(8,128)(2,1)S(1)}, u32[]{:S(2)}, u32[]{:S(2)}) collective-permute-start(bf16[224,896]{1,0:T(8,128)(2,1)S(1)} %broadcast_select_fusion.refs_0_), channel_id=1, source_target_pairs={{0,96},{16,112},{1,97},{17,113},{2,98},{18,114},{3,99},{19,115},{4... | collective-permute-start | bytes 1204232 | tf_op jit(solution)/shard_map/ppermute | solution.py:61
  42.9 15.7 %collective-permute-start.14 = (bf16[224,1152]{1,0:T(8,128)(2,1)S(1)}, bf16[224,1152]{1,0:T(8,128)(2,1)S(1)}, u32[]{:S(2)}, u32[]{:S(2)}) collective-permute-start(bf16[224,1152]{1,0:T(8,128)(2,1)S(1)} %collective-permute-done.8.in_ref), channel_id=1, source_target_pairs={{0,8},{16,24},{1,9},{17,25},{2,10},{18,26},{3,11},{19,27},{4,12},{... | collective-permute-start | bytes 1548296 | tf_op jit(solution)/shard_map/ppermute | solution.py:61
  47.6 12.3 %collective-permute-start.11 = (bf16[224,896]{1,0:T(8,128)(2,1)S(1)}, bf16[224,896]{1,0:T(8,128)(2,1)}, u32[]{:S(2)}, u32[]{:S(2)}) collective-permute-start(bf16[224,896]{1,0:T(8,128)(2,1)S(1)} %collective-permute-done.3.refs_4_), channel_id=1, source_target_pairs={{0,32},{16,48},{1,33},{17,49},{2,34},{18,50},{3,35},{19,51},{4,36}... | collective-permute-start | bytes 1204232 | tf_op jit(solution)/shard_map/ppermute | solution.py:61
  48.5 11.4 %collective-permute-start.12 = (bf16[224,896]{1,0:T(8,128)(2,1)S(1)}, bf16[224,896]{1,0:T(8,128)(2,1)S(1)}, u32[]{:S(2)}, u32[]{:S(2)}) collective-permute-start(bf16[224,896]{1,0:T(8,128)(2,1)S(1)} %collective-permute-done.6.refs_2_), channel_id=1, source_target_pairs={{0,96},{16,112},{1,97},{17,113},{2,98},{18,114},{3,99},{19,115},{4... | collective-permute-start | bytes 1204232 | tf_op jit(solution)/shard_map/ppermute | solution.py:61
  50.9 9.0 %collective-permute-start.13 = (bf16[224,896]{1,0:T(8,128)(2,1)S(1)}, bf16[224,896]{1,0:T(8,128)(2,1)}, u32[]{:S(2)}, u32[]{:S(2)}) collective-permute-start(bf16[224,896]{1,0:T(8,128)(2,1)S(1)} %broadcast_select_fusion.1.refs_0_), channel_id=1, source_target_pairs={{0,16},{16,0},{1,17},{17,1},{2,18},{18,2},{3,19},{19,3},{4,20},{20... | collective-permute-start | bytes 1204232 | tf_op jit(solution)/shard_map/ppermute | solution.py:61
  60.1 9.3 %collective-permute-start.19 = (bf16[224,896]{1,0:T(8,128)(2,1)S(1)}, bf16[224,896]{1,0:T(8,128)(2,1)S(1)}, u32[]{:S(2)}, u32[]{:S(2)}) collective-permute-start(bf16[224,896]{1,0:T(8,128)(2,1)S(1)} %collective-permute-done.12.refs_6_), channel_id=1, source_target_pairs={{0,16},{16,0},{1,17},{17,1},{2,18},{18,2},{3,19},{19,3},{4,20},{20... | collective-permute-start | bytes 1204232 | tf_op jit(solution)/shard_map/ppermute | solution.py:61
  62.0 8.7 %collective-permute-start.16 = (bf16[224,896]{1,0:T(8,128)(2,1)S(1)}, bf16[224,896]{1,0:T(8,128)(2,1)S(1)}, u32[]{:S(2)}, u32[]{:S(2)}) collective-permute-start(bf16[224,896]{1,0:T(8,128)(2,1)S(1)} %broadcast_select_fusion.refs_0_), channel_id=1, source_target_pairs={{0,16},{16,0},{1,17},{17,1},{2,18},{18,2},{3,19},{19,3},{4,20},{20... | collective-permute-start | bytes 1204232 | tf_op jit(solution)/shard_map/ppermute | solution.py:61
  62.2 8.6 %collective-permute-start.17 = (bf16[224,896]{1,0:T(8,128)(2,1)S(1)}, bf16[224,896]{1,0:T(8,128)(2,1)S(1)}, u32[]{:S(2)}, u32[]{:S(2)}) collective-permute-start(bf16[224,896]{1,0:T(8,128)(2,1)S(1)} %collective-permute-done.6.refs_2_), channel_id=1, source_target_pairs={{0,16},{16,0},{1,17},{17,1},{2,18},{18,2},{3,19},{19,3},{4,20},{20... | collective-permute-start | bytes 1204232 | tf_op jit(solution)/shard_map/ppermute | solution.py:61
  68.6 9.9 %collective-permute-start.20 = (bf16[112,896]{1,0:T(8,128)(2,1)}, bf16[112,896]{1,0:T(8,128)(2,1)S(1)}, u32[]{:S(2)}, u32[]{:S(2)}) collective-permute-start(bf16[112,896]{1,0:T(8,128)(2,1)} %get-tuple-element.74), channel_id=1, source_target_pairs={{0,8},{16,24},{1,9},{17,25},{2,10},{18,26},{3,11},{19,27},{4,12},{... | collective-permute-start | bytes 602120 | tf_op jit(solution)/shard_map/ppermute | solution.py:61
  69.4 12.5 %collective-permute-start.23 = (bf16[112,896]{1,0:T(8,128)(2,1)}, bf16[112,896]{1,0:T(8,128)(2,1)S(1)}, u32[]{:S(2)}, u32[]{:S(2)}) collective-permute-start(bf16[112,896]{1,0:T(8,128)(2,1)} %get-tuple-element.78), channel_id=1, source_target_pairs={{0,8},{16,24},{1,9},{17,25},{2,10},{18,26},{3,11},{19,27},{4,12},{... | collective-permute-start | bytes 602120 | tf_op jit(solution)/shard_map/ppermute | solution.py:61
  79.7 11.2 %collective-permute-start.21 = (bf16[112,896]{1,0:T(8,128)(2,1)S(1)}, bf16[112,896]{1,0:T(8,128)(2,1)S(1)}, u32[]{:S(2)}, u32[]{:S(2)}) collective-permute-start(bf16[112,896]{1,0:T(8,128)(2,1)S(1)} %get-tuple-element.75.refs_0_), channel_id=1, source_target_pairs={{0,1},{16,17},{1,2},{17,18},{2,3},{18,19},{3,4},{19,20},{4,5},{20,... | collective-permute-start | bytes 602120 | tf_op jit(solution)/shard_map/ppermute | solution.py:61
  83.1 10.0 %collective-permute-start.30 = (bf16[112,896]{1,0:T(8,128)(2,1)S(1)}, bf16[112,896]{1,0:T(8,128)(2,1)S(1)}, u32[]{:S(2)}, u32[]{:S(2)}) collective-permute-start(bf16[112,896]{1,0:T(8,128)(2,1)S(1)} %get-tuple-element.83.refs_0_), channel_id=1, source_target_pairs={{0,7},{16,23},{1,0},{17,16},{2,1},{18,17},{3,2},{19,18},{4,3},{20,... | collective-permute-start | bytes 602120 | tf_op jit(solution)/shard_map/ppermute | solution.py:61
  87.7 10.1 %collective-permute-start.24 = (bf16[112,896]{1,0:T(8,128)(2,1)S(1)}, bf16[112,896]{1,0:T(8,128)(2,1)S(1)}, u32[]{:S(2)}, u32[]{:S(2)}) collective-permute-start(bf16[112,896]{1,0:T(8,128)(2,1)S(1)} %get-tuple-element.75.refs_0_), channel_id=1, source_target_pairs={{0,7},{16,23},{1,0},{17,16},{2,1},{18,17},{3,2},{19,18},{4,3},{20,... | collective-permute-start | bytes 602120 | tf_op jit(solution)/shard_map/ppermute | solution.py:61
  90.9 10.2 %collective-permute-start.22 = (bf16[112,896]{1,0:T(8,128)(2,1)S(1)}, bf16[112,896]{1,0:T(8,128)(2,1)S(1)}, u32[]{:S(2)}, u32[]{:S(2)}) collective-permute-start(bf16[112,896]{1,0:T(8,128)(2,1)S(1)} %collective-permute-done.21.refs_7_), channel_id=1, source_target_pairs={{0,1},{16,17},{1,2},{17,18},{2,3},{18,19},{3,4},{19,20},{4,5},{20,... | collective-permute-start | bytes 602120 | tf_op jit(solution)/shard_map/ppermute | solution.py:61
  90.9 12.2 %collective-permute-start.34 = (bf16[112,896]{1,0:T(8,128)(2,1)S(1)}, bf16[112,896]{1,0:T(8,128)(2,1)S(1)}, u32[]{:S(2)}, u32[]{:S(2)}) collective-permute-start(bf16[112,896]{1,0:T(8,128)(2,1)S(1)} %get-tuple-element.83.refs_0_), channel_id=1, source_target_pairs={{0,1},{16,17},{1,2},{17,18},{2,3},{18,19},{3,4},{19,20},{4,5},{20,... | collective-permute-start | bytes 602120 | tf_op jit(solution)/shard_map/ppermute | solution.py:61
  93.1 9.9 %collective-permute-start.31 = (bf16[112,896]{1,0:T(8,128)(2,1)S(1)}, bf16[112,896]{1,0:T(8,128)(2,1)S(1)}, u32[]{:S(2)}, u32[]{:S(2)}) collective-permute-start(bf16[112,896]{1,0:T(8,128)(2,1)S(1)} %collective-permute-done.30.refs_1_), channel_id=1, source_target_pairs={{0,7},{16,23},{1,0},{17,16},{2,1},{18,17},{3,2},{19,18},{4,3},{20,... | collective-permute-start | bytes 602120 | tf_op jit(solution)/shard_map/ppermute | solution.py:61
  103.0 9.4 %collective-permute-start.35 = (bf16[112,896]{1,0:T(8,128)(2,1)S(1)}, bf16[112,896]{1,0:T(8,128)(2,1)S(1)}, u32[]{:S(2)}, u32[]{:S(2)}) collective-permute-start(bf16[112,896]{1,0:T(8,128)(2,1)S(1)} %collective-permute-done.34.refs_7_), channel_id=1, source_target_pairs={{0,1},{16,17},{1,2},{17,18},{2,3},{18,19},{3,4},{19,20},{4,5},{20,... | collective-permute-start | bytes 602120 | tf_op jit(solution)/shard_map/ppermute | solution.py:61
  103.0 9.4 %collective-permute-start.32 = (bf16[112,896]{1,0:T(8,128)(2,1)S(1)}, bf16[112,896]{1,0:T(8,128)(2,1)S(1)}, u32[]{:S(2)}, u32[]{:S(2)}) collective-permute-start(bf16[112,896]{1,0:T(8,128)(2,1)S(1)} %collective-permute-done.31.refs_2_), channel_id=1, source_target_pairs={{0,7},{16,23},{1,0},{17,16},{2,1},{18,17},{3,2},{19,18},{4,3},{20,... | collective-permute-start | bytes 602120 | tf_op jit(solution)/shard_map/ppermute | solution.py:61
  106.3 9.4 %collective-permute-start.26 = (bf16[112,896]{1,0:T(8,128)(2,1)S(1)}, bf16[112,896]{1,0:T(8,128)(2,1)S(1)}, u32[]{:S(2)}, u32[]{:S(2)}) collective-permute-start(bf16[112,896]{1,0:T(8,128)(2,1)S(1)} %collective-permute-done.25.refs_2_), channel_id=1, source_target_pairs={{0,7},{16,23},{1,0},{17,16},{2,1},{18,17},{3,2},{19,18},{4,3},{20,... | collective-permute-start | bytes 602120 | tf_op jit(solution)/shard_map/ppermute | solution.py:61
  109.1 8.6 %collective-permute-start.28 = (bf16[112,896]{1,0:T(8,128)(2,1)S(1)}, bf16[112,896]{1,0:T(8,128)(2,1)S(1)}, u32[]{:S(2)}, u32[]{:S(2)}) collective-permute-start(bf16[112,896]{1,0:T(8,128)(2,1)S(1)} %collective-permute-done.27.refs_5_), channel_id=1, source_target_pairs={{0,1},{16,17},{1,2},{17,18},{2,3},{18,19},{3,4},{19,20},{4,5},{20,... | collective-permute-start | bytes 602120 | tf_op jit(solution)/shard_map/ppermute | solution.py:61
  112.4 10.9 %collective-permute-start.36 = (bf16[112,896]{1,0:T(8,128)(2,1)S(1)}, bf16[112,896]{1,0:T(8,128)(2,1)S(1)}, u32[]{:S(2)}, u32[]{:S(2)}) collective-permute-start(bf16[112,896]{1,0:T(8,128)(2,1)S(1)} %collective-permute-done.35.refs_6_), channel_id=1, source_target_pairs={{0,1},{16,17},{1,2},{17,18},{2,3},{18,19},{3,4},{19,20},{4,5},{20,... | collective-permute-start | bytes 602120 | tf_op jit(solution)/shard_map/ppermute | solution.py:61
  112.4 10.9 %collective-permute-start.33 = (bf16[112,896]{1,0:T(8,128)(2,1)S(1)}, bf16[112,896]{1,0:T(8,128)(2,1)S(1)}, u32[]{:S(2)}, u32[]{:S(2)}) collective-permute-start(bf16[112,896]{1,0:T(8,128)(2,1)S(1)} %collective-permute-done.32.refs_3_), channel_id=1, source_target_pairs={{0,7},{16,23},{1,0},{17,16},{2,1},{18,17},{3,2},{19,18},{4,3},{20,... | collective-permute-start | bytes 602120 | tf_op jit(solution)/shard_map/ppermute | solution.py:61
  (27 other events, 298.4 us)
Sparse Core Ops, SparseCore 0:
  10.4 48.4 all-gather.4
  61.3 53.1 all-gather.6

commit v2 on v1

--- a/solution.py
+++ b/solution.py
@@ -125,40 +125,20 @@
 
 
 def margin_kernel(slot, a_ref, *refs):
-    b_refs, outs, (a_buf, b_buf, sems) = refs[:8], refs[8:10], refs[10:]
+    b_refs, outs = refs[:8], refs[8:]
     row = lax.axis_index("row")
     x = lax.div(lax.rem(row, 8), 2)
     c = lax.rem(row, 2)
-    copies = []
-    for n, (t, u) in enumerate(OLD_ORDER):
+    total = None
+    for b_ref, (t, u) in zip(b_refs, OLD_ORDER):
         kb = lax.rem(x + t, 4) * 2 + (c if u == 0 else 1 - c)
-        copies.append(
-            (
-                pltpu.make_async_copy(a_ref.at[kb], a_buf.at[n], sems.at[0, n]),
-                pltpu.make_async_copy(b_refs[n], b_buf.at[n], sems.at[1, n]),
-            )
-        )
-    for pair in copies:
-        for priority, copy in enumerate(pair):
-            copy.start(priority=priority)
-    total = None
-    for n, pair in enumerate(copies):
-        for copy in pair:
-            copy.wait()
         term = jnp.dot(
-            unpacked(a_buf[n]), unpacked(b_buf[n]), preferred_element_type=jnp.float32
+            unpacked(a_ref[kb]), unpacked(b_ref[...]), preferred_element_type=jnp.float32
         )
         total = term if total is None else total + term
     for half, out_ref in enumerate(outs):
         part = total[half * HALF : (half + 1) * HALF]
         out_ref[...] = packed(part.astype(jnp.bfloat16)) if slot == 0 else part
-
-
-MARGIN_SCRATCH = (
-    pltpu.VMEM((8, HALF, 2 * B), jnp.bfloat16),
-    pltpu.VMEM((8, HALF, 2 * B), jnp.bfloat16),
-    pltpu.SemaphoreType.DMA((2, 8)),
-)
 
 
 def margin_sum_kernel(keep_ref, other_ref, margin_ref, out_ref):
@@ -272,18 +252,12 @@
         [((QUARTER, 2 * B), bf16)] * 2,
         [a_all, o0, o0c, o0a, o0ac, o0b, o0bc, o0f, o0fc],
         flops=2 * B * B * 8 * B,
-        space=pl.ANY,
-        scratch=MARGIN_SCRATCH,
-        grant=58,
     )
     keeps = call(
         functools.partial(margin_kernel, 1),
         [((HALF, B), f32)] * 2,
         [a_all, o1, o1c, o1a, o1ac, o1b, o1bc, o1f, o1fc],
         flops=2 * B * B * 8 * B,
-        space=pl.ANY,
-        scratch=MARGIN_SCRATCH,
-        grant=58,
     )
     margins, halves = [], []
     for keep, other in zip(keeps, others):

time: 142 us -> 142 us (level)
  Pallas kernels: 24.5 us -> 18 us
  starting transfers between devices: 53.3 us -> 57.4 us
  waiting for transfers between devices: 40.3 us -> 43.7 us
    pallas_call x12, Pallas kernels: 24.5 us -> 18 us  [call(): pl.pallas_call(kernel, out_shape=shapes, in_specs=[pl.BlockSpec(memory_sp...]
    ppermute x38, starting transfers between devices: 53.2 us -> 57.3 us  [send(): return lax.ppermute(v, AXES, perm)]
    ppermute x38, waiting for transfers between devices: 40.2 us -> 43.7 us  [send(): return lax.ppermute(v, AXES, perm)]
    unnamed x38 -> x12, local copies, waits for them, and re-layouts: 7.95 us -> 7.02 us
  transfers between devices with their start and end apart: 40 -> 40, of which waited for: 17 -> 19; matrix products, arithmetic and copies ran while one was open for 1% -> 1% of each run, Pallas kernels for 15% -> 10%
where the time goes in v2:
time: 142 us
  starting transfers between devices  57.4 us (40%)
  waiting for transfers between devices  43.7 us (31%)
  Pallas kernels  18 us (13%)
  between operations  14.3 us (10%)
  local copies, waits for them, and re-layouts  7.02 us (5%)
    ppermute x38, starting transfers between devices, send(): return lax.ppermute(v, AXES, perm)  57.3 us
    ppermute x38, waiting for transfers between devices, send(): return lax.ppermute(v, AXES, perm)  43.7 us
    pallas_call x12, Pallas kernels, call(): pl.pallas_call(kernel, out_shape=shapes, in_specs=[pl.BlockSpec(memory_sp...  18 us
    unnamed x12, local copies, waits for them, and re-layouts  7.02 us
  transfers between devices with their start and end apart: 40, of which 19 were waited for; matrix products, arithmetic and copies ran while one was open for 1% of the time, Pallas kernels for 10%

profile of v2, /device:TPU:8, one launch (start us, length us, event | category | flops | bytes accessed | tf_op | source)
XLA Modules:
  0.0 141.5 jit_solution(5735035038560294035)
XLA Ops:
  7.2 2.6 %shard_map.59 = (bf16[224,896]{1,0:T(8,128)(2,1)}, bf16[224,896]{1,0:T(8,128)(2,1)}) custom-call(f32[448,448]{1,0:T(8,128)} %new_hbm.1, bf16[448,448]{1,0:T(8,128)(2,1)} %codes_hbm.1, f32[56,448]{1,0:T(8,128)} %scales_hbm.1), custom_call_target="tpu_custom_call" | custom-call | bytes 2107392 | tf_op jit(solution)/shard_map/pallas_call | solution.py:71
  11.5 3.8 %collective-permute-start.1 = (bf16[224,896]{1,0:T(8,128)(2,1)}, bf16[224,896]{1,0:T(8,128)(2,1)S(1)}, u32[]{:S(2)}, u32[]{:S(2)}) collective-permute-start(bf16[224,896]{1,0:T(8,128)(2,1)} %get-tuple-element.43), channel_id=1, source_target_pairs={{8,0},{24,16},{9,1},{25,17},{10,2},{26,18},{11,3},{27,19},{12,4},{... | collective-permute-start | bytes 1204232 | tf_op jit(solution)/shard_map/ppermute | solution.py:61
  15.4 5.8 %collective-permute-done = bf16[224,896]{1,0:T(8,128)(2,1)S(1)} collective-permute-done((bf16[224,896]{1,0:T(8,128)(2,1)}, bf16[224,896]{1,0:T(8,128)(2,1)S(1)}, u32[]{:S(2)}, u32[]{:S(2)}) %collective-permute-start) | collective-permute-done | bytes 401440 | tf_op jit(solution)/shard_map/ppermute | solution.py:61
  21.2 2.7 %collective-permute-done.1 = bf16[224,896]{1,0:T(8,128)(2,1)S(1)} collective-permute-done((bf16[224,896]{1,0:T(8,128)(2,1)}, bf16[224,896]{1,0:T(8,128)(2,1)S(1)}, u32[]{:S(2)}, u32[]{:S(2)}) %collective-permute-start.1) | collective-permute-done | bytes 401440 | tf_op jit(solution)/shard_map/ppermute | solution.py:61
  26.8 1.7 %collective-permute-start.4 = (bf16[224,896]{1,0:T(8,128)(2,1)S(1)}, bf16[224,896]{1,0:T(8,128)(2,1)S(1)}, u32[]{:S(2)}, u32[]{:S(2)}) collective-permute-start(bf16[224,896]{1,0:T(8,128)(2,1)S(1)} %broadcast_select_fusion.1.refs_0_), channel_id=1, source_target_pairs={{0,96},{16,112},{1,97},{17,113},{2,98},{18,114},{3,99},{19,115},{4... | collective-permute-start | bytes 1204232 | tf_op jit(solution)/shard_map/ppermute | solution.py:61
  28.8 4.9 %collective-permute-start.7 = (bf16[224,1152]{1,0:T(8,128)(2,1)S(1)}, bf16[224,1152]{1,0:T(8,128)(2,1)S(1)}, u32[]{:S(2)}, u32[]{:S(2)}) collective-permute-start(bf16[224,1152]{1,0:T(8,128)(2,1)S(1)} %shard_map.60.own_ref), channel_id=1, source_target_pairs={{8,0},{24,16},{9,1},{25,17},{10,2},{26,18},{11,3},{27,19},{12,4},{... | collective-permute-start | bytes 1548296 | tf_op jit(solution)/shard_map/ppermute | solution.py:61
  33.7 1.9 %collective-permute-done.2 = bf16[224,896]{1,0:T(8,128)(2,1)S(1)} collective-permute-done((bf16[224,896]{1,0:T(8,128)(2,1)S(1)}, bf16[224,896]{1,0:T(8,128)(2,1)S(1)}, u32[]{:S(2)}, u32[]{:S(2)}) %collective-permute-start.2) | collective-permute-done | bytes 401440 | tf_op jit(solution)/shard_map/ppermute | solution.py:61
  38.0 1.7 %collective-permute-start.6 = (bf16[224,896]{1,0:T(8,128)(2,1)S(1)}, bf16[224,896]{1,0:T(8,128)(2,1)S(1)}, u32[]{:S(2)}, u32[]{:S(2)}) collective-permute-start(bf16[224,896]{1,0:T(8,128)(2,1)S(1)} %broadcast_select_fusion.refs_0_), channel_id=1, source_target_pairs={{0,96},{16,112},{1,97},{17,113},{2,98},{18,114},{3,99},{19,115},{4... | collective-permute-start | bytes 1204232 | tf_op jit(solution)/shard_map/ppermute | solution.py:61
  40.5 1.8 %collective-permute-done.7.out_ref = bf16[224,1152]{1,0:T(8,128)(2,1)S(1)} collective-permute-done((bf16[224,1152]{1,0:T(8,128)(2,1)S(1)}, bf16[224,1152]{1,0:T(8,128)(2,1)S(1)}, u32[]{:S(2)}, u32[]{:S(2)}) %collective-permute-start.7) | collective-permute-done | bytes 516128 | tf_op jit(solution)/shard_map/ppermute | solution.py:61
  44.2 2.6 %collective-permute-done.5.refs_4_ = bf16[224,896]{1,0:T(8,128)(2,1)S(1)} collective-permute-done((bf16[224,896]{1,0:T(8,128)(2,1)S(1)}, bf16[224,896]{1,0:T(8,128)(2,1)S(1)}, u32[]{:S(2)}, u32[]{:S(2)}) %collective-permute-start.5) | collective-permute-done | bytes 401440 | tf_op jit(solution)/shard_map/ppermute | solution.py:61
  48.4 2.3 %collective-permute-start.12 = (bf16[224,896]{1,0:T(8,128)(2,1)S(1)}, bf16[224,896]{1,0:T(8,128)(2,1)S(1)}, u32[]{:S(2)}, u32[]{:S(2)}) collective-permute-start(bf16[224,896]{1,0:T(8,128)(2,1)S(1)} %collective-permute-done.6.refs_2_), channel_id=1, source_target_pairs={{0,96},{16,112},{1,97},{17,113},{2,98},{18,114},{3,99},{19,115},{4... | collective-permute-start | bytes 1204232 | tf_op jit(solution)/shard_map/ppermute | solution.py:61
  50.8 7.8 %collective-permute-done.14.relay_ref = bf16[224,1152]{1,0:T(8,128)(2,1)S(1)} collective-permute-done((bf16[224,1152]{1,0:T(8,128)(2,1)S(1)}, bf16[224,1152]{1,0:T(8,128)(2,1)S(1)}, u32[]{:S(2)}, u32[]{:S(2)}) %collective-permute-start.14) | collective-permute-done | bytes 516128 | tf_op jit(solution)/shard_map/ppermute | solution.py:61
  62.6 1.9 %copy-done.1 = bf16[1792,896]{1,0:T(8,128)(2,1)S(1)} copy-done((bf16[1792,896]{1,0:T(8,128)(2,1)S(1)}, bf16[1792,896]{1,0:T(8,128)(2,1)}, u32[]{:S(2)}) %copy-start.1) | copy-done | bytes 3211288
  65.5 3.3 %shard_map.63 = (bf16[112,896]{1,0:T(8,128)(2,1)S(1)}, bf16[112,896]{1,0:T(8,128)(2,1)S(1)}) custom-call(bf16[8,224,896]{2,1,0:T(8,128)(2,1)S(1)} %bitcast.9, bf16[224,896]{1,0:T(8,128)(2,1)S(1)} %broadcast_select_fusion.1.refs_0_, bf16[224,896]{1,0:T(8,128)(2,1)} %collective-permute-done.13.refs_1_, bf16[224,896]{1,0:T(8,128)(2,1)S(1)} %collective-permute-done.4.refs_2_, ...), custom_call_target="tpu_custom_call" | custom-call | flops 1438646272 | bytes 6823936 | tf_op jit(solution)/shard_map/pallas_call | solution.py:71
  71.0 2.1 %shard_map.62 = (f32[224,448]{1,0:T(8,128)S(1)}, f32[224,448]{1,0:T(8,128)S(1)}) custom-call(bf16[8,224,896]{2,1,0:T(8,128)(2,1)S(1)} %bitcast.10, bf16[224,896]{1,0:T(8,128)(2,1)S(1)} %broadcast_select_fusion.refs_0_, bf16[224,896]{1,0:T(8,128)(2,1)S(1)} %collective-permute-done.16.refs_1_, bf16[224,896]{1,0:T(8,128)(2,1)S(1)} %collective-permute-done.6.refs_2_, ...), custom_call_target="tpu_custom_call" | custom-call | flops 1438646272 | bytes 7225344 | tf_op jit(solution)/shard_map/pallas_call | solution.py:71
  73.1 3.6 %collective-permute-done.20.other_ref = bf16[112,896]{1,0:T(8,128)(2,1)S(1)} collective-permute-done((bf16[112,896]{1,0:T(8,128)(2,1)S(1)}, bf16[112,896]{1,0:T(8,128)(2,1)S(1)}, u32[]{:S(2)}, u32[]{:S(2)}) %collective-permute-start.20) | collective-permute-done | bytes 200736 | tf_op jit(solution)/shard_map/ppermute | solution.py:61
  76.9 2.1 %collective-permute-start.21 = (bf16[112,896]{1,0:T(8,128)(2,1)S(1)}, bf16[112,896]{1,0:T(8,128)(2,1)S(1)}, u32[]{:S(2)}, u32[]{:S(2)}) collective-permute-start(bf16[112,896]{1,0:T(8,128)(2,1)S(1)} %get-tuple-element.75.refs_0_), channel_id=1, source_target_pairs={{0,1},{16,17},{1,2},{17,18},{2,3},{18,19},{3,4},{19,20},{4,5},{20,... | collective-permute-start | bytes 602120 | tf_op jit(solution)/shard_map/ppermute | solution.py:61
  80.7 6.1 %collective-permute-start.30 = (bf16[112,896]{1,0:T(8,128)(2,1)S(1)}, bf16[112,896]{1,0:T(8,128)(2,1)S(1)}, u32[]{:S(2)}, u32[]{:S(2)}) collective-permute-start(bf16[112,896]{1,0:T(8,128)(2,1)S(1)} %get-tuple-element.83.refs_0_), channel_id=1, source_target_pairs={{0,7},{16,23},{1,0},{17,16},{2,1},{18,17},{3,2},{19,18},{4,3},{20,... | collective-permute-start | bytes 602120 | tf_op jit(solution)/shard_map/ppermute | solution.py:61
  88.8 3.4 %collective-permute-done.30.refs_1_ = bf16[112,896]{1,0:T(8,128)(2,1)S(1)} collective-permute-done((bf16[112,896]{1,0:T(8,128)(2,1)S(1)}, bf16[112,896]{1,0:T(8,128)(2,1)S(1)}, u32[]{:S(2)}, u32[]{:S(2)}) %collective-permute-start.30) | collective-permute-done | bytes 200736 | tf_op jit(solution)/shard_map/ppermute | solution.py:61
  92.2 3.7 %collective-permute-start.31 = (bf16[112,896]{1,0:T(8,128)(2,1)S(1)}, bf16[112,896]{1,0:T(8,128)(2,1)S(1)}, u32[]{:S(2)}, u32[]{:S(2)}) collective-permute-start(bf16[112,896]{1,0:T(8,128)(2,1)S(1)} %collective-permute-done.30.refs_1_), channel_id=1, source_target_pairs={{0,7},{16,23},{1,0},{17,16},{2,1},{18,17},{3,2},{19,18},{4,3},{20,... | collective-permute-start | bytes 602120 | tf_op jit(solution)/shard_map/ppermute | solution.py:61
  96.9 3.3 %collective-permute-start.25 = (bf16[112,896]{1,0:T(8,128)(2,1)S(1)}, bf16[112,896]{1,0:T(8,128)(2,1)S(1)}, u32[]{:S(2)}, u32[]{:S(2)}) collective-permute-start(bf16[112,896]{1,0:T(8,128)(2,1)S(1)} %collective-permute-done.24.refs_1_), channel_id=1, source_target_pairs={{0,7},{16,23},{1,0},{17,16},{2,1},{18,17},{3,2},{19,18},{4,3},{20,... | collective-permute-start | bytes 602120 | tf_op jit(solution)/shard_map/ppermute | solution.py:61
  101.1 3.7 %collective-permute-start.32 = (bf16[112,896]{1,0:T(8,128)(2,1)S(1)}, bf16[112,896]{1,0:T(8,128)(2,1)S(1)}, u32[]{:S(2)}, u32[]{:S(2)}) collective-permute-start(bf16[112,896]{1,0:T(8,128)(2,1)S(1)} %collective-permute-done.31.refs_2_), channel_id=1, source_target_pairs={{0,7},{16,23},{1,0},{17,16},{2,1},{18,17},{3,2},{19,18},{4,3},{20,... | collective-permute-start | bytes 602120 | tf_op jit(solution)/shard_map/ppermute | solution.py:61
  105.6 3.7 %collective-permute-start.26 = (bf16[112,896]{1,0:T(8,128)(2,1)S(1)}, bf16[112,896]{1,0:T(8,128)(2,1)S(1)}, u32[]{:S(2)}, u32[]{:S(2)}) collective-permute-start(bf16[112,896]{1,0:T(8,128)(2,1)S(1)} %collective-permute-done.25.refs_2_), channel_id=1, source_target_pairs={{0,7},{16,23},{1,0},{17,16},{2,1},{18,17},{3,2},{19,18},{4,3},{20,... | collective-permute-start | bytes 602120 | tf_op jit(solution)/shard_map/ppermute | solution.py:61
  110.2 3.7 %collective-permute-start.33 = (bf16[112,896]{1,0:T(8,128)(2,1)S(1)}, bf16[112,896]{1,0:T(8,128)(2,1)S(1)}, u32[]{:S(2)}, u32[]{:S(2)}) collective-permute-start(bf16[112,896]{1,0:T(8,128)(2,1)S(1)} %collective-permute-done.32.refs_3_), channel_id=1, source_target_pairs={{0,7},{16,23},{1,0},{17,16},{2,1},{18,17},{3,2},{19,18},{4,3},{20,... | collective-permute-start | bytes 602120 | tf_op jit(solution)/shard_map/ppermute | solution.py:61
  114.5 1.8 %collective-permute-done.28.refs_4_ = bf16[112,896]{1,0:T(8,128)(2,1)S(1)} collective-permute-done((bf16[112,896]{1,0:T(8,128)(2,1)S(1)}, bf16[112,896]{1,0:T(8,128)(2,1)S(1)}, u32[]{:S(2)}, u32[]{:S(2)}) %collective-permute-start.28) | collective-permute-done | bytes 200736 | tf_op jit(solution)/shard_map/ppermute | solution.py:61
  116.2 3.3 %copy-done = bf16[3584,1152]{1,0:T(8,128)(2,1)S(1)} copy-done((bf16[3584,1152]{1,0:T(8,128)(2,1)S(1)}, bf16[3584,1152]{1,0:T(8,128)(2,1)}, u32[]{:S(2)}) %copy-start) | copy-done | bytes 8257560
  119.6 1.7 %shard_map.67 = bf16[112,1152]{1,0:T(8,128)(2,1)S(1)} custom-call(bf16[8,448,1152]{2,1,0:T(8,128)(2,1)S(1)} %bitcast.5, bf16[112,896]{1,0:T(8,128)(2,1)S(1)} %get-tuple-element.75.refs_0_, bf16[112,896]{1,0:T(8,128)(2,1)S(1)} %collective-permute-done.24.refs_1_, bf16[112,896]{1,0:T(8,128)(2,1)S(1)} %collective-permute-done.25.refs_2_, ...), custom_call_target="tpu_custom_call" | custom-call | flops 924844032 | bytes 10121216 | tf_op jit(solution)/shard_map/pallas_call | solution.py:71
  122.1 1.7 %shard_map.69 = bf16[112,1152]{1,0:T(8,128)(2,1)S(1)} custom-call(bf16[8,448,1152]{2,1,0:T(8,128)(2,1)S(1)} %bitcast.6, bf16[112,896]{1,0:T(8,128)(2,1)S(1)} %get-tuple-element.83.refs_0_, bf16[112,896]{1,0:T(8,128)(2,1)S(1)} %collective-permute-done.30.refs_1_, bf16[112,896]{1,0:T(8,128)(2,1)S(1)} %collective-permute-done.31.refs_2_, ...), custom_call_target="tpu_custom_call" | custom-call | flops 924844032 | bytes 10121216 | tf_op jit(solution)/shard_map/pallas_call | solution.py:71
  125.2 1.8 %shard_map.66.keep_a = f32[224,576]{1,0:T(8,128)S(1)} custom-call(bf16[8,448,1152]{2,1,0:T(8,128)(2,1)S(1)} %bitcast.7, bf16[112,896]{1,0:T(8,128)(2,1)S(1)} %get-tuple-element.75.refs_0_, bf16[112,896]{1,0:T(8,128)(2,1)S(1)} %collective-permute-done.24.refs_1_, bf16[112,896]{1,0:T(8,128)(2,1)S(1)} %collective-permute-done.25.refs_2_, ...), custom_call_target="tpu_custom_call" | custom-call | flops 924844032 | bytes 10379264 | tf_op jit(solution)/shard_map/pallas_call | solution.py:71
  127.0 1.8 %shard_map.68.keep_b = f32[224,576]{1,0:T(8,128)S(1)} custom-call(bf16[8,448,1152]{2,1,0:T(8,128)(2,1)S(1)} %bitcast.8, bf16[112,896]{1,0:T(8,128)(2,1)S(1)} %get-tuple-element.83.refs_0_, bf16[112,896]{1,0:T(8,128)(2,1)S(1)} %collective-permute-done.30.refs_1_, bf16[112,896]{1,0:T(8,128)(2,1)S(1)} %collective-permute-done.31.refs_2_, ...), custom_call_target="tpu_custom_call" | custom-call | flops 924844032 | bytes 10379264 | tf_op jit(solution)/shard_map/pallas_call | solution.py:71
  128.8 1.7 %collective-permute-done.29.other_a = bf16[112,1152]{1,0:T(8,128)(2,1)S(1)} collective-permute-done((bf16[112,1152]{1,0:T(8,128)(2,1)S(1)}, bf16[112,1152]{1,0:T(8,128)(2,1)S(1)}, u32[]{:S(2)}, u32[]{:S(2)}) %collective-permute-start.29) | collective-permute-done | bytes 258080 | tf_op jit(solution)/shard_map/ppermute | solution.py:61
  130.5 3.0 %collective-permute-done.37.other_b = bf16[112,1152]{1,0:T(8,128)(2,1)S(1)} collective-permute-done((bf16[112,1152]{1,0:T(8,128)(2,1)S(1)}, bf16[112,1152]{1,0:T(8,128)(2,1)S(1)}, u32[]{:S(2)}, u32[]{:S(2)}) %collective-permute-start.37) | collective-permute-done | bytes 258080 | tf_op jit(solution)/shard_map/ppermute | solution.py:61
  (77 shorter events, 30.2 us)
Async XLA Ops:
  7.2 52.8 %all-gather.5.cloned.1.call-start = ((), (), s32[]{:S(2)}) async-start(), calls=%async_computation | async-start | bytes 3612672 | tf_op jit(solution)/shard_map/all_gather | solution.py:224
  9.8 106.4 %all-gather.7.cloned.1.call-start = ((), (), s32[]{:S(2)}) async-start(), calls=%async_computation.1 | async-start | bytes 9289728 | tf_op jit(solution)/shard_map/all_gather | solution.py:244
  9.9 11.3 %collective-permute-start = (bf16[224,896]{1,0:T(8,128)(2,1)}, bf16[224,896]{1,0:T(8,128)(2,1)S(1)}, u32[]{:S(2)}, u32[]{:S(2)}) collective-permute-start(bf16[224,896]{1,0:T(8,128)(2,1)} %get-tuple-element.43), channel_id=1, source_target_pairs={{0,136},{16,152},{1,137},{17,153},{2,138},{18,154},{3,139},{19,155... | collective-permute-start | bytes 1204232 | tf_op jit(solution)/shard_map/ppermute | solution.py:61
  11.5 12.4 %collective-permute-start.1 = (bf16[224,896]{1,0:T(8,128)(2,1)}, bf16[224,896]{1,0:T(8,128)(2,1)S(1)}, u32[]{:S(2)}, u32[]{:S(2)}) collective-permute-start(bf16[224,896]{1,0:T(8,128)(2,1)} %get-tuple-element.43), channel_id=1, source_target_pairs={{8,0},{24,16},{9,1},{25,17},{10,2},{26,18},{11,3},{27,19},{12,4},{... | collective-permute-start | bytes 1204232 | tf_op jit(solution)/shard_map/ppermute | solution.py:61
  23.9 11.7 %collective-permute-start.2 = (bf16[224,896]{1,0:T(8,128)(2,1)S(1)}, bf16[224,896]{1,0:T(8,128)(2,1)S(1)}, u32[]{:S(2)}, u32[]{:S(2)}) collective-permute-start(bf16[224,896]{1,0:T(8,128)(2,1)S(1)} %collective-permute-done), channel_id=1, source_target_pairs={{0,8},{16,24},{1,9},{17,25},{2,10},{18,26},{3,11},{19,27},{4,12},{... | collective-permute-start | bytes 1204232 | tf_op jit(solution)/shard_map/ppermute | solution.py:61
  25.2 11.1 %collective-permute-start.3 = (bf16[224,896]{1,0:T(8,128)(2,1)S(1)}, bf16[224,896]{1,0:T(8,128)(2,1)S(1)}, u32[]{:S(2)}, u32[]{:S(2)}) collective-permute-start(bf16[224,896]{1,0:T(8,128)(2,1)S(1)} %broadcast_select_fusion.1.refs_0_), channel_id=1, source_target_pairs={{0,32},{16,48},{1,33},{17,49},{2,34},{18,50},{3,35},{19,51},{4,36}... | collective-permute-start | bytes 1204232 | tf_op jit(solution)/shard_map/ppermute | solution.py:61
  26.8 9.6 %collective-permute-start.4 = (bf16[224,896]{1,0:T(8,128)(2,1)S(1)}, bf16[224,896]{1,0:T(8,128)(2,1)S(1)}, u32[]{:S(2)}, u32[]{:S(2)}) collective-permute-start(bf16[224,896]{1,0:T(8,128)(2,1)S(1)} %broadcast_select_fusion.1.refs_0_), channel_id=1, source_target_pairs={{0,96},{16,112},{1,97},{17,113},{2,98},{18,114},{3,99},{19,115},{4... | collective-permute-start | bytes 1204232 | tf_op jit(solution)/shard_map/ppermute | solution.py:61
  28.7 11.8 %collective-permute-start.8 = (bf16[224,1152]{1,0:T(8,128)(2,1)S(1)}, bf16[224,1152]{1,0:T(8,128)(2,1)S(1)}, u32[]{:S(2)}, u32[]{:S(2)}) collective-permute-start(bf16[224,1152]{1,0:T(8,128)(2,1)S(1)} %shard_map.60.own_ref), channel_id=1, source_target_pairs={{0,136},{16,152},{1,137},{17,153},{2,138},{18,154},{3,139},{19,155... | collective-permute-start | bytes 1548296 | tf_op jit(solution)/shard_map/ppermute | solution.py:61
  28.8 13.6 %collective-permute-start.7 = (bf16[224,1152]{1,0:T(8,128)(2,1)S(1)}, bf16[224,1152]{1,0:T(8,128)(2,1)S(1)}, u32[]{:S(2)}, u32[]{:S(2)}) collective-permute-start(bf16[224,1152]{1,0:T(8,128)(2,1)S(1)} %shard_map.60.own_ref), channel_id=1, source_target_pairs={{8,0},{24,16},{9,1},{25,17},{10,2},{26,18},{11,3},{27,19},{12,4},{... | collective-permute-start | bytes 1548296 | tf_op jit(solution)/shard_map/ppermute | solution.py:61
  36.4 10.3 %collective-permute-start.5 = (bf16[224,896]{1,0:T(8,128)(2,1)S(1)}, bf16[224,896]{1,0:T(8,128)(2,1)S(1)}, u32[]{:S(2)}, u32[]{:S(2)}) collective-permute-start(bf16[224,896]{1,0:T(8,128)(2,1)S(1)} %broadcast_select_fusion.refs_0_), channel_id=1, source_target_pairs={{0,32},{16,48},{1,33},{17,49},{2,34},{18,50},{3,35},{19,51},{4,36}... | collective-permute-start | bytes 1204232 | tf_op jit(solution)/shard_map/ppermute | solution.py:61
  42.9 15.7 %collective-permute-start.14 = (bf16[224,1152]{1,0:T(8,128)(2,1)S(1)}, bf16[224,1152]{1,0:T(8,128)(2,1)S(1)}, u32[]{:S(2)}, u32[]{:S(2)}) collective-permute-start(bf16[224,1152]{1,0:T(8,128)(2,1)S(1)} %collective-permute-done.8.in_ref), channel_id=1, source_target_pairs={{0,8},{16,24},{1,9},{17,25},{2,10},{18,26},{3,11},{19,27},{4,12},{... | collective-permute-start | bytes 1548296 | tf_op jit(solution)/shard_map/ppermute | solution.py:61
  47.5 12.4 %collective-permute-start.11 = (bf16[224,896]{1,0:T(8,128)(2,1)S(1)}, bf16[224,896]{1,0:T(8,128)(2,1)}, u32[]{:S(2)}, u32[]{:S(2)}) collective-permute-start(bf16[224,896]{1,0:T(8,128)(2,1)S(1)} %collective-permute-done.3.refs_4_), channel_id=1, source_target_pairs={{0,32},{16,48},{1,33},{17,49},{2,34},{18,50},{3,35},{19,51},{4,36}... | collective-permute-start | bytes 1204232 | tf_op jit(solution)/shard_map/ppermute | solution.py:61
  48.4 11.5 %collective-permute-start.12 = (bf16[224,896]{1,0:T(8,128)(2,1)S(1)}, bf16[224,896]{1,0:T(8,128)(2,1)S(1)}, u32[]{:S(2)}, u32[]{:S(2)}) collective-permute-start(bf16[224,896]{1,0:T(8,128)(2,1)S(1)} %collective-permute-done.6.refs_2_), channel_id=1, source_target_pairs={{0,96},{16,112},{1,97},{17,113},{2,98},{18,114},{3,99},{19,115},{4... | collective-permute-start | bytes 1204232 | tf_op jit(solution)/shard_map/ppermute | solution.py:61
  50.8 9.1 %collective-permute-start.13 = (bf16[224,896]{1,0:T(8,128)(2,1)S(1)}, bf16[224,896]{1,0:T(8,128)(2,1)}, u32[]{:S(2)}, u32[]{:S(2)}) collective-permute-start(bf16[224,896]{1,0:T(8,128)(2,1)S(1)} %broadcast_select_fusion.1.refs_0_), channel_id=1, source_target_pairs={{0,16},{16,0},{1,17},{17,1},{2,18},{18,2},{3,19},{19,3},{4,20},{20... | collective-permute-start | bytes 1204232 | tf_op jit(solution)/shard_map/ppermute | solution.py:61
  60.0 9.6 %collective-permute-start.19 = (bf16[224,896]{1,0:T(8,128)(2,1)S(1)}, bf16[224,896]{1,0:T(8,128)(2,1)S(1)}, u32[]{:S(2)}, u32[]{:S(2)}) collective-permute-start(bf16[224,896]{1,0:T(8,128)(2,1)S(1)} %collective-permute-done.12.refs_6_), channel_id=1, source_target_pairs={{0,16},{16,0},{1,17},{17,1},{2,18},{18,2},{3,19},{19,3},{4,20},{20... | collective-permute-start | bytes 1204232 | tf_op jit(solution)/shard_map/ppermute | solution.py:61
  62.0 9.0 %collective-permute-start.16 = (bf16[224,896]{1,0:T(8,128)(2,1)S(1)}, bf16[224,896]{1,0:T(8,128)(2,1)S(1)}, u32[]{:S(2)}, u32[]{:S(2)}) collective-permute-start(bf16[224,896]{1,0:T(8,128)(2,1)S(1)} %broadcast_select_fusion.refs_0_), channel_id=1, source_target_pairs={{0,16},{16,0},{1,17},{17,1},{2,18},{18,2},{3,19},{19,3},{4,20},{20... | collective-permute-start | bytes 1204232 | tf_op jit(solution)/shard_map/ppermute | solution.py:61
  62.1 8.9 %collective-permute-start.17 = (bf16[224,896]{1,0:T(8,128)(2,1)S(1)}, bf16[224,896]{1,0:T(8,128)(2,1)S(1)}, u32[]{:S(2)}, u32[]{:S(2)}) collective-permute-start(bf16[224,896]{1,0:T(8,128)(2,1)S(1)} %collective-permute-done.6.refs_2_), channel_id=1, source_target_pairs={{0,16},{16,0},{1,17},{17,1},{2,18},{18,2},{3,19},{19,3},{4,20},{20... | collective-permute-start | bytes 1204232 | tf_op jit(solution)/shard_map/ppermute | solution.py:61
  69.6 10.9 %collective-permute-start.23 = (bf16[112,896]{1,0:T(8,128)(2,1)S(1)}, bf16[112,896]{1,0:T(8,128)(2,1)S(1)}, u32[]{:S(2)}, u32[]{:S(2)}) collective-permute-start(bf16[112,896]{1,0:T(8,128)(2,1)S(1)} %get-tuple-element.78), channel_id=1, source_target_pairs={{0,8},{16,24},{1,9},{17,25},{2,10},{18,26},{3,11},{19,27},{4,12},{... | collective-permute-start | bytes 602120 | tf_op jit(solution)/shard_map/ppermute | solution.py:61
  76.9 10.8 %collective-permute-start.21 = (bf16[112,896]{1,0:T(8,128)(2,1)S(1)}, bf16[112,896]{1,0:T(8,128)(2,1)S(1)}, u32[]{:S(2)}, u32[]{:S(2)}) collective-permute-start(bf16[112,896]{1,0:T(8,128)(2,1)S(1)} %get-tuple-element.75.refs_0_), channel_id=1, source_target_pairs={{0,1},{16,17},{1,2},{17,18},{2,3},{18,19},{3,4},{19,20},{4,5},{20,... | collective-permute-start | bytes 602120 | tf_op jit(solution)/shard_map/ppermute | solution.py:61
  80.7 11.5 %collective-permute-start.30 = (bf16[112,896]{1,0:T(8,128)(2,1)S(1)}, bf16[112,896]{1,0:T(8,128)(2,1)S(1)}, u32[]{:S(2)}, u32[]{:S(2)}) collective-permute-start(bf16[112,896]{1,0:T(8,128)(2,1)S(1)} %get-tuple-element.83.refs_0_), channel_id=1, source_target_pairs={{0,7},{16,23},{1,0},{17,16},{2,1},{18,17},{3,2},{19,18},{4,3},{20,... | collective-permute-start | bytes 602120 | tf_op jit(solution)/shard_map/ppermute | solution.py:61
  86.8 10.1 %collective-permute-start.24 = (bf16[112,896]{1,0:T(8,128)(2,1)S(1)}, bf16[112,896]{1,0:T(8,128)(2,1)S(1)}, u32[]{:S(2)}, u32[]{:S(2)}) collective-permute-start(bf16[112,896]{1,0:T(8,128)(2,1)S(1)} %get-tuple-element.75.refs_0_), channel_id=1, source_target_pairs={{0,7},{16,23},{1,0},{17,16},{2,1},{18,17},{3,2},{19,18},{4,3},{20,... | collective-permute-start | bytes 602120 | tf_op jit(solution)/shard_map/ppermute | solution.py:61
  87.7 12.4 %collective-permute-start.22 = (bf16[112,896]{1,0:T(8,128)(2,1)S(1)}, bf16[112,896]{1,0:T(8,128)(2,1)S(1)}, u32[]{:S(2)}, u32[]{:S(2)}) collective-permute-start(bf16[112,896]{1,0:T(8,128)(2,1)S(1)} %collective-permute-done.21.refs_7_), channel_id=1, source_target_pairs={{0,1},{16,17},{1,2},{17,18},{2,3},{18,19},{3,4},{19,20},{4,5},{20,... | collective-permute-start | bytes 602120 | tf_op jit(solution)/shard_map/ppermute | solution.py:61
  88.8 11.4 %collective-permute-start.34 = (bf16[112,896]{1,0:T(8,128)(2,1)S(1)}, bf16[112,896]{1,0:T(8,128)(2,1)S(1)}, u32[]{:S(2)}, u32[]{:S(2)}) collective-permute-start(bf16[112,896]{1,0:T(8,128)(2,1)S(1)} %get-tuple-element.83.refs_0_), channel_id=1, source_target_pairs={{0,1},{16,17},{1,2},{17,18},{2,3},{18,19},{3,4},{19,20},{4,5},{20,... | collective-permute-start | bytes 602120 | tf_op jit(solution)/shard_map/ppermute | solution.py:61
  92.2 8.9 %collective-permute-start.31 = (bf16[112,896]{1,0:T(8,128)(2,1)S(1)}, bf16[112,896]{1,0:T(8,128)(2,1)S(1)}, u32[]{:S(2)}, u32[]{:S(2)}) collective-permute-start(bf16[112,896]{1,0:T(8,128)(2,1)S(1)} %collective-permute-done.30.refs_1_), channel_id=1, source_target_pairs={{0,7},{16,23},{1,0},{17,16},{2,1},{18,17},{3,2},{19,18},{4,3},{20,... | collective-permute-start | bytes 602120 | tf_op jit(solution)/shard_map/ppermute | solution.py:61
  100.2 9.1 %collective-permute-start.27 = (bf16[112,896]{1,0:T(8,128)(2,1)S(1)}, bf16[112,896]{1,0:T(8,128)(2,1)S(1)}, u32[]{:S(2)}, u32[]{:S(2)}) collective-permute-start(bf16[112,896]{1,0:T(8,128)(2,1)S(1)} %collective-permute-done.22.refs_6_), channel_id=1, source_target_pairs={{0,1},{16,17},{1,2},{17,18},{2,3},{18,19},{3,4},{19,20},{4,5},{20,... | collective-permute-start | bytes 602120 | tf_op jit(solution)/shard_map/ppermute | solution.py:61
  100.2 10.1 %collective-permute-start.35 = (bf16[112,896]{1,0:T(8,128)(2,1)S(1)}, bf16[112,896]{1,0:T(8,128)(2,1)S(1)}, u32[]{:S(2)}, u32[]{:S(2)}) collective-permute-start(bf16[112,896]{1,0:T(8,128)(2,1)S(1)} %collective-permute-done.34.refs_7_), channel_id=1, source_target_pairs={{0,1},{16,17},{1,2},{17,18},{2,3},{18,19},{3,4},{19,20},{4,5},{20,... | collective-permute-start | bytes 602120 | tf_op jit(solution)/shard_map/ppermute | solution.py:61
  101.1 9.2 %collective-permute-start.32 = (bf16[112,896]{1,0:T(8,128)(2,1)S(1)}, bf16[112,896]{1,0:T(8,128)(2,1)S(1)}, u32[]{:S(2)}, u32[]{:S(2)}) collective-permute-start(bf16[112,896]{1,0:T(8,128)(2,1)S(1)} %collective-permute-done.31.refs_2_), channel_id=1, source_target_pairs={{0,7},{16,23},{1,0},{17,16},{2,1},{18,17},{3,2},{19,18},{4,3},{20,... | collective-permute-start | bytes 602120 | tf_op jit(solution)/shard_map/ppermute | solution.py:61
  105.6 8.8 %collective-permute-start.26 = (bf16[112,896]{1,0:T(8,128)(2,1)S(1)}, bf16[112,896]{1,0:T(8,128)(2,1)S(1)}, u32[]{:S(2)}, u32[]{:S(2)}) collective-permute-start(bf16[112,896]{1,0:T(8,128)(2,1)S(1)} %collective-permute-done.25.refs_2_), channel_id=1, source_target_pairs={{0,7},{16,23},{1,0},{17,16},{2,1},{18,17},{3,2},{19,18},{4,3},{20,... | collective-permute-start | bytes 602120 | tf_op jit(solution)/shard_map/ppermute | solution.py:61
  110.2 11.8 %collective-permute-start.36 = (bf16[112,896]{1,0:T(8,128)(2,1)S(1)}, bf16[112,896]{1,0:T(8,128)(2,1)S(1)}, u32[]{:S(2)}, u32[]{:S(2)}) collective-permute-start(bf16[112,896]{1,0:T(8,128)(2,1)S(1)} %collective-permute-done.35.refs_6_), channel_id=1, source_target_pairs={{0,1},{16,17},{1,2},{17,18},{2,3},{18,19},{3,4},{19,20},{4,5},{20,... | collective-permute-start | bytes 602120 | tf_op jit(solution)/shard_map/ppermute | solution.py:61
  110.2 11.8 %collective-permute-start.33 = (bf16[112,896]{1,0:T(8,128)(2,1)S(1)}, bf16[112,896]{1,0:T(8,128)(2,1)S(1)}, u32[]{:S(2)}, u32[]{:S(2)}) collective-permute-start(bf16[112,896]{1,0:T(8,128)(2,1)S(1)} %collective-permute-done.32.refs_3_), channel_id=1, source_target_pairs={{0,7},{16,23},{1,0},{17,16},{2,1},{18,17},{3,2},{19,18},{4,3},{20,... | collective-permute-start | bytes 602120 | tf_op jit(solution)/shard_map/ppermute | solution.py:61
  121.3 9.2 %collective-permute-start.29 = (bf16[112,1152]{1,0:T(8,128)(2,1)S(1)}, bf16[112,1152]{1,0:T(8,128)(2,1)S(1)}, u32[]{:S(2)}, u32[]{:S(2)}) collective-permute-start(bf16[112,1152]{1,0:T(8,128)(2,1)S(1)} %shard_map.67), channel_id=1, source_target_pairs={{0,8},{16,24},{1,9},{17,25},{2,10},{18,26},{3,11},{19,27},{4,12},{... | collective-permute-start | bytes 774152 | tf_op jit(solution)/shard_map/ppermute | solution.py:61
  123.8 9.7 %collective-permute-start.37 = (bf16[112,1152]{1,0:T(8,128)(2,1)S(1)}, bf16[112,1152]{1,0:T(8,128)(2,1)S(1)}, u32[]{:S(2)}, u32[]{:S(2)}) collective-permute-start(bf16[112,1152]{1,0:T(8,128)(2,1)S(1)} %shard_map.69), channel_id=1, source_target_pairs={{0,8},{16,24},{1,9},{17,25},{2,10},{18,26},{3,11},{19,27},{4,12},{... | collective-permute-start | bytes 774152 | tf_op jit(solution)/shard_map/ppermute | solution.py:61
  (14 other events, 106.6 us)
Sparse Core Ops, SparseCore 0:
  10.4 48.4 all-gather.4
  61.3 53.0 all-gather.6

commit v3 on v2

--- a/solution.py
+++ b/solution.py
@@ -55,6 +55,7 @@
 Y_SWAP = y_perm(Y_SWAP_TO, (0, 1, 2, 3))
 Y_OUT = y_perm(Y_OUT_TO, (1, 2))
 Y_RELAY = y_perm(Y_OUT_TO, (0, 3))
+Y_BOTH = y_perm(Y_OUT_TO, (0, 1, 2, 3))
 
 
 def send(v, perm):
@@ -151,7 +152,7 @@
     out_ref[...] = packed(moment_ref[...].astype(jnp.bfloat16))
 
 
-def moment_pair_kernel(own_ref, in_ref, out_ref, relay_ref, pair_ref):
+def moment_pair_kernel(own_ref, in_ref, out_ref, pair_ref):
     edge = lax.div(lax.axis_index("col"), 8) == lax.div(lax.axis_index("row"), 8)
     width = pair_ref.shape[1] // 2
 
@@ -163,7 +164,7 @@
     @pl.when(jnp.logical_not(edge))
     def _():
         pair_ref[:, :width] = unpacked(in_ref[...])
-        pair_ref[:, width:] = unpacked(relay_ref[...])
+        pair_ref[:, width:] = unpacked(out_ref[...])
 
 
 def rotate_kernel(slot, b_ref, *refs):
@@ -229,17 +230,17 @@
     o0 = jnp.where(edge, o_out, o_in)
     o_relay, o0b, o0a = send(o_in, Y_RELAY), send(o0, X_UP), send(o0, X_DOWN)
     (m,) = call(moment_kernel, [((HALF, 2 * width), bf16)], [moment])
-    m_in, m_out = send(m, Y_SWAP), send(m, Y_OUT)
+    m_in = send(m, Y_SWAP)
     o_relay, o0b, o0a = rounds(o_relay, o0b, o0a)
     o1 = jnp.where(edge, o, o_relay)
     o1b, o1a = send(o1, X_UP), send(o1, X_DOWN)
     m_in, o0a_, o0b_ = rounds(m_in, o0a, o0b)
-    m_out, o0a_, o0b_ = rounds(m_out, o0a_, o0b_)
-    o0ac, o0bc, m_relay = send(o0a_, CORE), send(o0b_, CORE), send(m_in, Y_RELAY)
+    m_out = send(jnp.where(edge, m_in, m), Y_BOTH)
+    o0ac, o0bc = send(o0a_, CORE), send(o0b_, CORE)
     o1b, o1a, o0b, o0, o0ac, o0bc = rounds(o1b, o1a, o0b, o0, o0ac, o0bc)
     o0f, o1f = send(o0b, X_UP), send(o1a, X_DOWN)
     o0c = send(o0, CORE)
-    (m01,) = call(moment_pair_kernel, [((B, 2 * width), bf16)], [m, m_in, m_out, m_relay])
+    (m01,) = call(moment_pair_kernel, [((B, 2 * width), bf16)], [m, m_in, m_out])
     o0f, o1f, o0c, m01 = rounds(o0f, o1f, o0c, m01)
     m_all = lax.all_gather(m01, "row", axis_index_groups=groups8)
     o0f, o1f, a_all = rounds(o0f, o1f, a_all)

time: 142 us -> 139 us (0.979)
  starting transfers between devices: 57.4 us -> 52.2 us
  waiting for transfers between devices: 43.7 us -> 46.1 us
    ppermute x38 -> x37, starting transfers between devices: 57.3 us -> 52.1 us  [send(): return lax.ppermute(v, AXES, perm)]
    ppermute x38 -> x37, waiting for transfers between devices: 43.7 us -> 45.3 us  [send(): return lax.ppermute(v, AXES, perm)]
  transfers between devices with their start and end apart: 40 -> 39, of which waited for: 19 -> 19; matrix products, arithmetic and copies ran while one was open for 1% -> 1% of each run, Pallas kernels for 10% -> 10%
where the time goes in v3:
time: 139 us
  starting transfers between devices  52.2 us (38%)
  waiting for transfers between devices  46.1 us (33%)
  Pallas kernels  18 us (13%)
  between operations  14.2 us (10%)
  local copies, waits for them, and re-layouts  7.02 us (5%)
    ppermute x37, starting transfers between devices, send(): return lax.ppermute(v, AXES, perm)  52.1 us
    ppermute x37, waiting for transfers between devices, send(): return lax.ppermute(v, AXES, perm)  45.3 us
    pallas_call x12, Pallas kernels, call(): pl.pallas_call(kernel, out_shape=shapes, in_specs=[pl.BlockSpec(memory_sp...  18 us
    unnamed x12, local copies, waits for them, and re-layouts  7.02 us
  transfers between devices with their start and end apart: 39, of which 19 were waited for; matrix products, arithmetic and copies ran while one was open for 1% of the time, Pallas kernels for 10%

profile of v3, /device:TPU:8, one launch (start us, length us, event | category | flops | bytes accessed | tf_op | source)
XLA Modules:
  0.0 138.7 jit_solution(13355674827391776281)
XLA Ops:
  7.2 2.6 %shard_map.59 = (bf16[224,896]{1,0:T(8,128)(2,1)}, bf16[224,896]{1,0:T(8,128)(2,1)}) custom-call(f32[448,448]{1,0:T(8,128)} %new_hbm.1, bf16[448,448]{1,0:T(8,128)(2,1)} %codes_hbm.1, f32[56,448]{1,0:T(8,128)} %scales_hbm.1), custom_call_target="tpu_custom_call" | custom-call | bytes 2107392 | tf_op jit(solution)/shard_map/pallas_call | solution.py:72
  11.5 3.8 %collective-permute-start.1 = (bf16[224,896]{1,0:T(8,128)(2,1)}, bf16[224,896]{1,0:T(8,128)(2,1)S(1)}, u32[]{:S(2)}, u32[]{:S(2)}) collective-permute-start(bf16[224,896]{1,0:T(8,128)(2,1)} %get-tuple-element.40), channel_id=1, source_target_pairs={{8,0},{24,16},{9,1},{25,17},{10,2},{26,18},{11,3},{27,19},{12,4},{... | collective-permute-start | bytes 1204232 | tf_op jit(solution)/shard_map/ppermute | solution.py:62
  15.4 5.8 %collective-permute-done = bf16[224,896]{1,0:T(8,128)(2,1)S(1)} collective-permute-done((bf16[224,896]{1,0:T(8,128)(2,1)}, bf16[224,896]{1,0:T(8,128)(2,1)S(1)}, u32[]{:S(2)}, u32[]{:S(2)}) %collective-permute-start) | collective-permute-done | bytes 401440 | tf_op jit(solution)/shard_map/ppermute | solution.py:62
  21.2 2.7 %collective-permute-done.1 = bf16[224,896]{1,0:T(8,128)(2,1)S(1)} collective-permute-done((bf16[224,896]{1,0:T(8,128)(2,1)}, bf16[224,896]{1,0:T(8,128)(2,1)S(1)}, u32[]{:S(2)}, u32[]{:S(2)}) %collective-permute-start.1) | collective-permute-done | bytes 401440 | tf_op jit(solution)/shard_map/ppermute | solution.py:62
  26.8 1.7 %collective-permute-start.4 = (bf16[224,896]{1,0:T(8,128)(2,1)S(1)}, bf16[224,896]{1,0:T(8,128)(2,1)S(1)}, u32[]{:S(2)}, u32[]{:S(2)}) collective-permute-start(bf16[224,896]{1,0:T(8,128)(2,1)S(1)} %broadcast_select_fusion.2.refs_0_), channel_id=1, source_target_pairs={{0,96},{16,112},{1,97},{17,113},{2,98},{18,114},{3,99},{19,115},{4... | collective-permute-start | bytes 1204232 | tf_op jit(solution)/shard_map/ppermute | solution.py:62
  28.8 6.8 %collective-permute-done.2 = bf16[224,896]{1,0:T(8,128)(2,1)S(1)} collective-permute-done((bf16[224,896]{1,0:T(8,128)(2,1)S(1)}, bf16[224,896]{1,0:T(8,128)(2,1)S(1)}, u32[]{:S(2)}, u32[]{:S(2)}) %collective-permute-start.2) | collective-permute-done | bytes 401440 | tf_op jit(solution)/shard_map/ppermute | solution.py:62
  38.0 1.7 %collective-permute-start.6 = (bf16[224,896]{1,0:T(8,128)(2,1)S(1)}, bf16[224,896]{1,0:T(8,128)(2,1)S(1)}, u32[]{:S(2)}, u32[]{:S(2)}) collective-permute-start(bf16[224,896]{1,0:T(8,128)(2,1)S(1)} %broadcast_select_fusion.1.refs_0_), channel_id=1, source_target_pairs={{0,96},{16,112},{1,97},{17,113},{2,98},{18,114},{3,99},{19,115},{4... | collective-permute-start | bytes 1204232 | tf_op jit(solution)/shard_map/ppermute | solution.py:62
  41.1 3.7 %collective-permute-start.13 = (bf16[224,1152]{1,0:T(8,128)(2,1)S(1)}, bf16[224,1152]{1,0:T(8,128)(2,1)S(1)}, u32[]{:S(2)}, u32[]{:S(2)}) collective-permute-start(bf16[224,1152]{1,0:T(8,128)(2,1)S(1)} %broadcast_select_fusion), channel_id=1, source_target_pairs={{0,8},{16,24},{1,9},{17,25},{2,10},{18,26},{3,11},{19,27},{4,12},{... | collective-permute-start | bytes 1548296 | tf_op jit(solution)/shard_map/ppermute | solution.py:62
  44.8 1.9 %collective-permute-done.5.refs_4_ = bf16[224,896]{1,0:T(8,128)(2,1)S(1)} collective-permute-done((bf16[224,896]{1,0:T(8,128)(2,1)S(1)}, bf16[224,896]{1,0:T(8,128)(2,1)S(1)}, u32[]{:S(2)}, u32[]{:S(2)}) %collective-permute-start.5) | collective-permute-done | bytes 401440 | tf_op jit(solution)/shard_map/ppermute | solution.py:62
  48.4 2.3 %collective-permute-start.11 = (bf16[224,896]{1,0:T(8,128)(2,1)S(1)}, bf16[224,896]{1,0:T(8,128)(2,1)S(1)}, u32[]{:S(2)}, u32[]{:S(2)}) collective-permute-start(bf16[224,896]{1,0:T(8,128)(2,1)S(1)} %collective-permute-done.6.refs_2_), channel_id=1, source_target_pairs={{0,96},{16,112},{1,97},{17,113},{2,98},{18,114},{3,99},{19,115},{4... | collective-permute-start | bytes 1204232 | tf_op jit(solution)/shard_map/ppermute | solution.py:62
  50.8 6.0 %collective-permute-done.13.out_ref = bf16[224,1152]{1,0:T(8,128)(2,1)S(1)} collective-permute-done((bf16[224,1152]{1,0:T(8,128)(2,1)S(1)}, bf16[224,1152]{1,0:T(8,128)(2,1)S(1)}, u32[]{:S(2)}, u32[]{:S(2)}) %collective-permute-start.13) | collective-permute-done | bytes 516128 | tf_op jit(solution)/shard_map/ppermute | solution.py:62
  59.4 2.0 %collective-permute-done.14.refs_7_ = bf16[224,896]{1,0:T(8,128)(2,1)S(1)} collective-permute-done((bf16[224,896]{1,0:T(8,128)(2,1)}, bf16[224,896]{1,0:T(8,128)(2,1)S(1)}, u32[]{:S(2)}, u32[]{:S(2)}) %collective-permute-start.14) | collective-permute-done | bytes 401440 | tf_op jit(solution)/shard_map/ppermute | solution.py:62
  62.0 1.9 %copy-done.1 = bf16[1792,896]{1,0:T(8,128)(2,1)S(1)} copy-done((bf16[1792,896]{1,0:T(8,128)(2,1)S(1)}, bf16[1792,896]{1,0:T(8,128)(2,1)}, u32[]{:S(2)}) %copy-start.1) | copy-done | bytes 3211288
  64.9 3.3 %shard_map.63 = (bf16[112,896]{1,0:T(8,128)(2,1)S(1)}, bf16[112,896]{1,0:T(8,128)(2,1)S(1)}) custom-call(bf16[8,224,896]{2,1,0:T(8,128)(2,1)S(1)} %bitcast.9, bf16[224,896]{1,0:T(8,128)(2,1)S(1)} %broadcast_select_fusion.2.refs_0_, bf16[224,896]{1,0:T(8,128)(2,1)} %collective-permute-done.12.refs_1_, bf16[224,896]{1,0:T(8,128)(2,1)S(1)} %collective-permute-done.4.refs_2_, ...), custom_call_target="tpu_custom_call" | custom-call | flops 1438646272 | bytes 6823936 | tf_op jit(solution)/shard_map/pallas_call | solution.py:72
  70.4 2.1 %shard_map.62 = (f32[224,448]{1,0:T(8,128)S(1)}, f32[224,448]{1,0:T(8,128)S(1)}) custom-call(bf16[8,224,896]{2,1,0:T(8,128)(2,1)S(1)} %bitcast.10, bf16[224,896]{1,0:T(8,128)(2,1)S(1)} %broadcast_select_fusion.1.refs_0_, bf16[224,896]{1,0:T(8,128)(2,1)S(1)} %collective-permute-done.15.refs_1_, bf16[224,896]{1,0:T(8,128)(2,1)S(1)} %collective-permute-done.6.refs_2_, ...), custom_call_target="tpu_custom_call" | custom-call | flops 1438646272 | bytes 7225344 | tf_op jit(solution)/shard_map/pallas_call | solution.py:72
  72.5 3.6 %collective-permute-done.19.other_ref = bf16[112,896]{1,0:T(8,128)(2,1)S(1)} collective-permute-done((bf16[112,896]{1,0:T(8,128)(2,1)S(1)}, bf16[112,896]{1,0:T(8,128)(2,1)S(1)}, u32[]{:S(2)}, u32[]{:S(2)}) %collective-permute-start.19) | collective-permute-done | bytes 200736 | tf_op jit(solution)/shard_map/ppermute | solution.py:62
  77.1 2.8 %collective-permute-done.22.other_ref = bf16[112,896]{1,0:T(8,128)(2,1)S(1)} collective-permute-done((bf16[112,896]{1,0:T(8,128)(2,1)S(1)}, bf16[112,896]{1,0:T(8,128)(2,1)S(1)}, u32[]{:S(2)}, u32[]{:S(2)}) %collective-permute-start.22) | collective-permute-done | bytes 200736 | tf_op jit(solution)/shard_map/ppermute | solution.py:62
  80.1 4.9 %collective-permute-start.29 = (bf16[112,896]{1,0:T(8,128)(2,1)S(1)}, bf16[112,896]{1,0:T(8,128)(2,1)S(1)}, u32[]{:S(2)}, u32[]{:S(2)}) collective-permute-start(bf16[112,896]{1,0:T(8,128)(2,1)S(1)} %get-tuple-element.77.refs_0_), channel_id=1, source_target_pairs={{0,7},{16,23},{1,0},{17,16},{2,1},{18,17},{3,2},{19,18},{4,3},{20,... | collective-permute-start | bytes 602120 | tf_op jit(solution)/shard_map/ppermute | solution.py:62
  87.0 3.3 %collective-permute-done.29.refs_1_ = bf16[112,896]{1,0:T(8,128)(2,1)S(1)} collective-permute-done((bf16[112,896]{1,0:T(8,128)(2,1)S(1)}, bf16[112,896]{1,0:T(8,128)(2,1)S(1)}, u32[]{:S(2)}, u32[]{:S(2)}) %collective-permute-start.29) | collective-permute-done | bytes 200736 | tf_op jit(solution)/shard_map/ppermute | solution.py:62
  90.4 3.7 %collective-permute-start.30 = (bf16[112,896]{1,0:T(8,128)(2,1)S(1)}, bf16[112,896]{1,0:T(8,128)(2,1)S(1)}, u32[]{:S(2)}, u32[]{:S(2)}) collective-permute-start(bf16[112,896]{1,0:T(8,128)(2,1)S(1)} %collective-permute-done.29.refs_1_), channel_id=1, source_target_pairs={{0,7},{16,23},{1,0},{17,16},{2,1},{18,17},{3,2},{19,18},{4,3},{20,... | collective-permute-start | bytes 602120 | tf_op jit(solution)/shard_map/ppermute | solution.py:62
  95.1 3.3 %collective-permute-start.24 = (bf16[112,896]{1,0:T(8,128)(2,1)S(1)}, bf16[112,896]{1,0:T(8,128)(2,1)S(1)}, u32[]{:S(2)}, u32[]{:S(2)}) collective-permute-start(bf16[112,896]{1,0:T(8,128)(2,1)S(1)} %collective-permute-done.23.refs_1_), channel_id=1, source_target_pairs={{0,7},{16,23},{1,0},{17,16},{2,1},{18,17},{3,2},{19,18},{4,3},{20,... | collective-permute-start | bytes 602120 | tf_op jit(solution)/shard_map/ppermute | solution.py:62
  99.3 3.7 %collective-permute-start.31 = (bf16[112,896]{1,0:T(8,128)(2,1)S(1)}, bf16[112,896]{1,0:T(8,128)(2,1)S(1)}, u32[]{:S(2)}, u32[]{:S(2)}) collective-permute-start(bf16[112,896]{1,0:T(8,128)(2,1)S(1)} %collective-permute-done.30.refs_2_), channel_id=1, source_target_pairs={{0,7},{16,23},{1,0},{17,16},{2,1},{18,17},{3,2},{19,18},{4,3},{20,... | collective-permute-start | bytes 602120 | tf_op jit(solution)/shard_map/ppermute | solution.py:62
  103.8 3.7 %collective-permute-start.25 = (bf16[112,896]{1,0:T(8,128)(2,1)S(1)}, bf16[112,896]{1,0:T(8,128)(2,1)S(1)}, u32[]{:S(2)}, u32[]{:S(2)}) collective-permute-start(bf16[112,896]{1,0:T(8,128)(2,1)S(1)} %collective-permute-done.24.refs_2_), channel_id=1, source_target_pairs={{0,7},{16,23},{1,0},{17,16},{2,1},{18,17},{3,2},{19,18},{4,3},{20,... | collective-permute-start | bytes 602120 | tf_op jit(solution)/shard_map/ppermute | solution.py:62
  108.6 3.5 %collective-permute-start.32 = (bf16[112,896]{1,0:T(8,128)(2,1)S(1)}, bf16[112,896]{1,0:T(8,128)(2,1)S(1)}, u32[]{:S(2)}, u32[]{:S(2)}) collective-permute-start(bf16[112,896]{1,0:T(8,128)(2,1)S(1)} %collective-permute-done.31.refs_3_), channel_id=1, source_target_pairs={{0,7},{16,23},{1,0},{17,16},{2,1},{18,17},{3,2},{19,18},{4,3},{20,... | collective-permute-start | bytes 602120 | tf_op jit(solution)/shard_map/ppermute | solution.py:62
  112.7 1.8 %collective-permute-done.27.refs_4_ = bf16[112,896]{1,0:T(8,128)(2,1)S(1)} collective-permute-done((bf16[112,896]{1,0:T(8,128)(2,1)S(1)}, bf16[112,896]{1,0:T(8,128)(2,1)S(1)}, u32[]{:S(2)}, u32[]{:S(2)}) %collective-permute-start.27) | collective-permute-done | bytes 200736 | tf_op jit(solution)/shard_map/ppermute | solution.py:62
  114.6 3.3 %copy-done = bf16[3584,1152]{1,0:T(8,128)(2,1)S(1)} copy-done((bf16[3584,1152]{1,0:T(8,128)(2,1)S(1)}, bf16[3584,1152]{1,0:T(8,128)(2,1)}, u32[]{:S(2)}) %copy-start) | copy-done | bytes 8257560
  117.9 1.7 %shard_map.67 = bf16[112,1152]{1,0:T(8,128)(2,1)S(1)} custom-call(bf16[8,448,1152]{2,1,0:T(8,128)(2,1)S(1)} %bitcast.5, bf16[112,896]{1,0:T(8,128)(2,1)S(1)} %get-tuple-element.69.refs_0_, bf16[112,896]{1,0:T(8,128)(2,1)S(1)} %collective-permute-done.23.refs_1_, bf16[112,896]{1,0:T(8,128)(2,1)S(1)} %collective-permute-done.24.refs_2_, ...), custom_call_target="tpu_custom_call" | custom-call | flops 924844032 | bytes 10121216 | tf_op jit(solution)/shard_map/pallas_call | solution.py:72
  119.6 1.7 %collective-permute-start.28 = (bf16[112,1152]{1,0:T(8,128)(2,1)S(1)}, bf16[112,1152]{1,0:T(8,128)(2,1)S(1)}, u32[]{:S(2)}, u32[]{:S(2)}) collective-permute-start(bf16[112,1152]{1,0:T(8,128)(2,1)S(1)} %shard_map.67), channel_id=1, source_target_pairs={{0,8},{16,24},{1,9},{17,25},{2,10},{18,26},{3,11},{19,27},{4,12},{... | collective-permute-start | bytes 774152 | tf_op jit(solution)/shard_map/ppermute | solution.py:62
  121.3 1.7 %shard_map.69 = bf16[112,1152]{1,0:T(8,128)(2,1)S(1)} custom-call(bf16[8,448,1152]{2,1,0:T(8,128)(2,1)S(1)} %bitcast.6, bf16[112,896]{1,0:T(8,128)(2,1)S(1)} %get-tuple-element.77.refs_0_, bf16[112,896]{1,0:T(8,128)(2,1)S(1)} %collective-permute-done.29.refs_1_, bf16[112,896]{1,0:T(8,128)(2,1)S(1)} %collective-permute-done.30.refs_2_, ...), custom_call_target="tpu_custom_call" | custom-call | flops 924844032 | bytes 10121216 | tf_op jit(solution)/shard_map/pallas_call | solution.py:72
  123.5 1.8 %shard_map.66.keep_a = f32[224,576]{1,0:T(8,128)S(1)} custom-call(bf16[8,448,1152]{2,1,0:T(8,128)(2,1)S(1)} %bitcast.7, bf16[112,896]{1,0:T(8,128)(2,1)S(1)} %get-tuple-element.69.refs_0_, bf16[112,896]{1,0:T(8,128)(2,1)S(1)} %collective-permute-done.23.refs_1_, bf16[112,896]{1,0:T(8,128)(2,1)S(1)} %collective-permute-done.24.refs_2_, ...), custom_call_target="tpu_custom_call" | custom-call | flops 924844032 | bytes 10379264 | tf_op jit(solution)/shard_map/pallas_call | solution.py:72
  125.3 1.8 %shard_map.68.keep_b = f32[224,576]{1,0:T(8,128)S(1)} custom-call(bf16[8,448,1152]{2,1,0:T(8,128)(2,1)S(1)} %bitcast.8, bf16[112,896]{1,0:T(8,128)(2,1)S(1)} %get-tuple-element.77.refs_0_, bf16[112,896]{1,0:T(8,128)(2,1)S(1)} %collective-permute-done.29.refs_1_, bf16[112,896]{1,0:T(8,128)(2,1)S(1)} %collective-permute-done.30.refs_2_, ...), custom_call_target="tpu_custom_call" | custom-call | flops 924844032 | bytes 10379264 | tf_op jit(solution)/shard_map/pallas_call | solution.py:72
  127.9 2.8 %collective-permute-done.36.other_b = bf16[112,1152]{1,0:T(8,128)(2,1)S(1)} collective-permute-done((bf16[112,1152]{1,0:T(8,128)(2,1)S(1)}, bf16[112,1152]{1,0:T(8,128)(2,1)S(1)}, u32[]{:S(2)}, u32[]{:S(2)}) %collective-permute-start.36) | collective-permute-done | bytes 258080 | tf_op jit(solution)/shard_map/ppermute | solution.py:62
  (76 shorter events, 26.9 us)
Async XLA Ops:
  7.2 51.7 %all-gather.5.cloned.1.call-start = ((), (), s32[]{:S(2)}) async-start(), calls=%async_computation | async-start | bytes 3612672 | tf_op jit(solution)/shard_map/all_gather | solution.py:225
  9.8 104.7 %all-gather.7.cloned.1.call-start = ((), (), s32[]{:S(2)}) async-start(), calls=%async_computation.1 | async-start | bytes 9289728 | tf_op jit(solution)/shard_map/all_gather | solution.py:245
  9.9 11.3 %collective-permute-start = (bf16[224,896]{1,0:T(8,128)(2,1)}, bf16[224,896]{1,0:T(8,128)(2,1)S(1)}, u32[]{:S(2)}, u32[]{:S(2)}) collective-permute-start(bf16[224,896]{1,0:T(8,128)(2,1)} %get-tuple-element.40), channel_id=1, source_target_pairs={{0,136},{16,152},{1,137},{17,153},{2,138},{18,154},{3,139},{19,155... | collective-permute-start | bytes 1204232 | tf_op jit(solution)/shard_map/ppermute | solution.py:62
  11.5 12.4 %collective-permute-start.1 = (bf16[224,896]{1,0:T(8,128)(2,1)}, bf16[224,896]{1,0:T(8,128)(2,1)S(1)}, u32[]{:S(2)}, u32[]{:S(2)}) collective-permute-start(bf16[224,896]{1,0:T(8,128)(2,1)} %get-tuple-element.40), channel_id=1, source_target_pairs={{8,0},{24,16},{9,1},{25,17},{10,2},{26,18},{11,3},{27,19},{12,4},{... | collective-permute-start | bytes 1204232 | tf_op jit(solution)/shard_map/ppermute | solution.py:62
  23.9 11.7 %collective-permute-start.2 = (bf16[224,896]{1,0:T(8,128)(2,1)S(1)}, bf16[224,896]{1,0:T(8,128)(2,1)S(1)}, u32[]{:S(2)}, u32[]{:S(2)}) collective-permute-start(bf16[224,896]{1,0:T(8,128)(2,1)S(1)} %collective-permute-done), channel_id=1, source_target_pairs={{0,8},{16,24},{1,9},{17,25},{2,10},{18,26},{3,11},{19,27},{4,12},{... | collective-permute-start | bytes 1204232 | tf_op jit(solution)/shard_map/ppermute | solution.py:62
  25.2 11.1 %collective-permute-start.3 = (bf16[224,896]{1,0:T(8,128)(2,1)S(1)}, bf16[224,896]{1,0:T(8,128)(2,1)S(1)}, u32[]{:S(2)}, u32[]{:S(2)}) collective-permute-start(bf16[224,896]{1,0:T(8,128)(2,1)S(1)} %broadcast_select_fusion.2.refs_0_), channel_id=1, source_target_pairs={{0,32},{16,48},{1,33},{17,49},{2,34},{18,50},{3,35},{19,51},{4,36}... | collective-permute-start | bytes 1204232 | tf_op jit(solution)/shard_map/ppermute | solution.py:62
  26.8 9.6 %collective-permute-start.4 = (bf16[224,896]{1,0:T(8,128)(2,1)S(1)}, bf16[224,896]{1,0:T(8,128)(2,1)S(1)}, u32[]{:S(2)}, u32[]{:S(2)}) collective-permute-start(bf16[224,896]{1,0:T(8,128)(2,1)S(1)} %broadcast_select_fusion.2.refs_0_), channel_id=1, source_target_pairs={{0,96},{16,112},{1,97},{17,113},{2,98},{18,114},{3,99},{19,115},{4... | collective-permute-start | bytes 1204232 | tf_op jit(solution)/shard_map/ppermute | solution.py:62
  28.7 11.8 %collective-permute-start.7 = (bf16[224,1152]{1,0:T(8,128)(2,1)S(1)}, bf16[224,1152]{1,0:T(8,128)(2,1)S(1)}, u32[]{:S(2)}, u32[]{:S(2)}) collective-permute-start(bf16[224,1152]{1,0:T(8,128)(2,1)S(1)} %shard_map.60.own_ref), channel_id=1, source_target_pairs={{0,136},{16,152},{1,137},{17,153},{2,138},{18,154},{3,139},{19,155... | collective-permute-start | bytes 1548296 | tf_op jit(solution)/shard_map/ppermute | solution.py:62
  36.4 10.3 %collective-permute-start.5 = (bf16[224,896]{1,0:T(8,128)(2,1)S(1)}, bf16[224,896]{1,0:T(8,128)(2,1)S(1)}, u32[]{:S(2)}, u32[]{:S(2)}) collective-permute-start(bf16[224,896]{1,0:T(8,128)(2,1)S(1)} %broadcast_select_fusion.1.refs_0_), channel_id=1, source_target_pairs={{0,32},{16,48},{1,33},{17,49},{2,34},{18,50},{3,35},{19,51},{4,36}... | collective-permute-start | bytes 1204232 | tf_op jit(solution)/shard_map/ppermute | solution.py:62
  38.0 8.7 %collective-permute-start.6 = (bf16[224,896]{1,0:T(8,128)(2,1)S(1)}, bf16[224,896]{1,0:T(8,128)(2,1)S(1)}, u32[]{:S(2)}, u32[]{:S(2)}) collective-permute-start(bf16[224,896]{1,0:T(8,128)(2,1)S(1)} %broadcast_select_fusion.1.refs_0_), channel_id=1, source_target_pairs={{0,96},{16,112},{1,97},{17,113},{2,98},{18,114},{3,99},{19,115},{4... | collective-permute-start | bytes 1204232 | tf_op jit(solution)/shard_map/ppermute | solution.py:62
  41.1 15.6 %collective-permute-start.13 = (bf16[224,1152]{1,0:T(8,128)(2,1)S(1)}, bf16[224,1152]{1,0:T(8,128)(2,1)S(1)}, u32[]{:S(2)}, u32[]{:S(2)}) collective-permute-start(bf16[224,1152]{1,0:T(8,128)(2,1)S(1)} %broadcast_select_fusion), channel_id=1, source_target_pairs={{0,8},{16,24},{1,9},{17,25},{2,10},{18,26},{3,11},{19,27},{4,12},{... | collective-permute-start | bytes 1548296 | tf_op jit(solution)/shard_map/ppermute | solution.py:62
  47.5 10.6 %collective-permute-start.10 = (bf16[224,896]{1,0:T(8,128)(2,1)S(1)}, bf16[224,896]{1,0:T(8,128)(2,1)}, u32[]{:S(2)}, u32[]{:S(2)}) collective-permute-start(bf16[224,896]{1,0:T(8,128)(2,1)S(1)} %collective-permute-done.3.refs_4_), channel_id=1, source_target_pairs={{0,32},{16,48},{1,33},{17,49},{2,34},{18,50},{3,35},{19,51},{4,36}... | collective-permute-start | bytes 1204232 | tf_op jit(solution)/shard_map/ppermute | solution.py:62
  48.4 9.7 %collective-permute-start.11 = (bf16[224,896]{1,0:T(8,128)(2,1)S(1)}, bf16[224,896]{1,0:T(8,128)(2,1)S(1)}, u32[]{:S(2)}, u32[]{:S(2)}) collective-permute-start(bf16[224,896]{1,0:T(8,128)(2,1)S(1)} %collective-permute-done.6.refs_2_), channel_id=1, source_target_pairs={{0,96},{16,112},{1,97},{17,113},{2,98},{18,114},{3,99},{19,115},{4... | collective-permute-start | bytes 1204232 | tf_op jit(solution)/shard_map/ppermute | solution.py:62
  58.9 10.0 %collective-permute-start.18 = (bf16[224,896]{1,0:T(8,128)(2,1)S(1)}, bf16[224,896]{1,0:T(8,128)(2,1)S(1)}, u32[]{:S(2)}, u32[]{:S(2)}) collective-permute-start(bf16[224,896]{1,0:T(8,128)(2,1)S(1)} %collective-permute-done.11.refs_6_), channel_id=1, source_target_pairs={{0,16},{16,0},{1,17},{17,1},{2,18},{18,2},{3,19},{19,3},{4,20},{20... | collective-permute-start | bytes 1204232 | tf_op jit(solution)/shard_map/ppermute | solution.py:62
  61.4 9.0 %collective-permute-start.15 = (bf16[224,896]{1,0:T(8,128)(2,1)S(1)}, bf16[224,896]{1,0:T(8,128)(2,1)S(1)}, u32[]{:S(2)}, u32[]{:S(2)}) collective-permute-start(bf16[224,896]{1,0:T(8,128)(2,1)S(1)} %broadcast_select_fusion.1.refs_0_), channel_id=1, source_target_pairs={{0,16},{16,0},{1,17},{17,1},{2,18},{18,2},{3,19},{19,3},{4,20},{20... | collective-permute-start | bytes 1204232 | tf_op jit(solution)/shard_map/ppermute | solution.py:62
  61.5 8.9 %collective-permute-start.16 = (bf16[224,896]{1,0:T(8,128)(2,1)S(1)}, bf16[224,896]{1,0:T(8,128)(2,1)S(1)}, u32[]{:S(2)}, u32[]{:S(2)}) collective-permute-start(bf16[224,896]{1,0:T(8,128)(2,1)S(1)} %collective-permute-done.6.refs_2_), channel_id=1, source_target_pairs={{0,16},{16,0},{1,17},{17,1},{2,18},{18,2},{3,19},{19,3},{4,20},{20... | collective-permute-start | bytes 1204232 | tf_op jit(solution)/shard_map/ppermute | solution.py:62
  61.9 8.5 %collective-permute-start.17 = (bf16[224,896]{1,0:T(8,128)(2,1)S(1)}, bf16[224,896]{1,0:T(8,128)(2,1)S(1)}, u32[]{:S(2)}, u32[]{:S(2)}) collective-permute-start(bf16[224,896]{1,0:T(8,128)(2,1)S(1)} %collective-permute-done.5.refs_4_), channel_id=1, source_target_pairs={{0,16},{16,0},{1,17},{17,1},{2,18},{18,2},{3,19},{19,3},{4,20},{20... | collective-permute-start | bytes 1204232 | tf_op jit(solution)/shard_map/ppermute | solution.py:62
  68.9 11.0 %collective-permute-start.22 = (bf16[112,896]{1,0:T(8,128)(2,1)S(1)}, bf16[112,896]{1,0:T(8,128)(2,1)S(1)}, u32[]{:S(2)}, u32[]{:S(2)}) collective-permute-start(bf16[112,896]{1,0:T(8,128)(2,1)S(1)} %get-tuple-element.72), channel_id=1, source_target_pairs={{0,8},{16,24},{1,9},{17,25},{2,10},{18,26},{3,11},{19,27},{4,12},{... | collective-permute-start | bytes 602120 | tf_op jit(solution)/shard_map/ppermute | solution.py:62
  76.3 9.6 %collective-permute-start.20 = (bf16[112,896]{1,0:T(8,128)(2,1)S(1)}, bf16[112,896]{1,0:T(8,128)(2,1)S(1)}, u32[]{:S(2)}, u32[]{:S(2)}) collective-permute-start(bf16[112,896]{1,0:T(8,128)(2,1)S(1)} %get-tuple-element.69.refs_0_), channel_id=1, source_target_pairs={{0,1},{16,17},{1,2},{17,18},{2,3},{18,19},{3,4},{19,20},{4,5},{20,... | collective-permute-start | bytes 602120 | tf_op jit(solution)/shard_map/ppermute | solution.py:62
  80.1 10.3 %collective-permute-start.29 = (bf16[112,896]{1,0:T(8,128)(2,1)S(1)}, bf16[112,896]{1,0:T(8,128)(2,1)S(1)}, u32[]{:S(2)}, u32[]{:S(2)}) collective-permute-start(bf16[112,896]{1,0:T(8,128)(2,1)S(1)} %get-tuple-element.77.refs_0_), channel_id=1, source_target_pairs={{0,7},{16,23},{1,0},{17,16},{2,1},{18,17},{3,2},{19,18},{4,3},{20,... | collective-permute-start | bytes 602120 | tf_op jit(solution)/shard_map/ppermute | solution.py:62
  85.0 10.1 %collective-permute-start.23 = (bf16[112,896]{1,0:T(8,128)(2,1)S(1)}, bf16[112,896]{1,0:T(8,128)(2,1)S(1)}, u32[]{:S(2)}, u32[]{:S(2)}) collective-permute-start(bf16[112,896]{1,0:T(8,128)(2,1)S(1)} %get-tuple-element.69.refs_0_), channel_id=1, source_target_pairs={{0,7},{16,23},{1,0},{17,16},{2,1},{18,17},{3,2},{19,18},{4,3},{20,... | collective-permute-start | bytes 602120 | tf_op jit(solution)/shard_map/ppermute | solution.py:62
  86.0 12.4 %collective-permute-start.21 = (bf16[112,896]{1,0:T(8,128)(2,1)S(1)}, bf16[112,896]{1,0:T(8,128)(2,1)S(1)}, u32[]{:S(2)}, u32[]{:S(2)}) collective-permute-start(bf16[112,896]{1,0:T(8,128)(2,1)S(1)} %collective-permute-done.20.refs_7_), channel_id=1, source_target_pairs={{0,1},{16,17},{1,2},{17,18},{2,3},{18,19},{3,4},{19,20},{4,5},{20,... | collective-permute-start | bytes 602120 | tf_op jit(solution)/shard_map/ppermute | solution.py:62
  87.0 11.4 %collective-permute-start.33 = (bf16[112,896]{1,0:T(8,128)(2,1)S(1)}, bf16[112,896]{1,0:T(8,128)(2,1)S(1)}, u32[]{:S(2)}, u32[]{:S(2)}) collective-permute-start(bf16[112,896]{1,0:T(8,128)(2,1)S(1)} %get-tuple-element.77.refs_0_), channel_id=1, source_target_pairs={{0,1},{16,17},{1,2},{17,18},{2,3},{18,19},{3,4},{19,20},{4,5},{20,... | collective-permute-start | bytes 602120 | tf_op jit(solution)/shard_map/ppermute | solution.py:62
  90.4 8.9 %collective-permute-start.30 = (bf16[112,896]{1,0:T(8,128)(2,1)S(1)}, bf16[112,896]{1,0:T(8,128)(2,1)S(1)}, u32[]{:S(2)}, u32[]{:S(2)}) collective-permute-start(bf16[112,896]{1,0:T(8,128)(2,1)S(1)} %collective-permute-done.29.refs_1_), channel_id=1, source_target_pairs={{0,7},{16,23},{1,0},{17,16},{2,1},{18,17},{3,2},{19,18},{4,3},{20,... | collective-permute-start | bytes 602120 | tf_op jit(solution)/shard_map/ppermute | solution.py:62
  95.1 8.7 %collective-permute-start.24 = (bf16[112,896]{1,0:T(8,128)(2,1)S(1)}, bf16[112,896]{1,0:T(8,128)(2,1)S(1)}, u32[]{:S(2)}, u32[]{:S(2)}) collective-permute-start(bf16[112,896]{1,0:T(8,128)(2,1)S(1)} %collective-permute-done.23.refs_1_), channel_id=1, source_target_pairs={{0,7},{16,23},{1,0},{17,16},{2,1},{18,17},{3,2},{19,18},{4,3},{20,... | collective-permute-start | bytes 602120 | tf_op jit(solution)/shard_map/ppermute | solution.py:62
  98.4 9.1 %collective-permute-start.26 = (bf16[112,896]{1,0:T(8,128)(2,1)S(1)}, bf16[112,896]{1,0:T(8,128)(2,1)S(1)}, u32[]{:S(2)}, u32[]{:S(2)}) collective-permute-start(bf16[112,896]{1,0:T(8,128)(2,1)S(1)} %collective-permute-done.21.refs_6_), channel_id=1, source_target_pairs={{0,1},{16,17},{1,2},{17,18},{2,3},{18,19},{3,4},{19,20},{4,5},{20,... | collective-permute-start | bytes 602120 | tf_op jit(solution)/shard_map/ppermute | solution.py:62
  98.4 10.2 %collective-permute-start.34 = (bf16[112,896]{1,0:T(8,128)(2,1)S(1)}, bf16[112,896]{1,0:T(8,128)(2,1)S(1)}, u32[]{:S(2)}, u32[]{:S(2)}) collective-permute-start(bf16[112,896]{1,0:T(8,128)(2,1)S(1)} %collective-permute-done.33.refs_7_), channel_id=1, source_target_pairs={{0,1},{16,17},{1,2},{17,18},{2,3},{18,19},{3,4},{19,20},{4,5},{20,... | collective-permute-start | bytes 602120 | tf_op jit(solution)/shard_map/ppermute | solution.py:62
  99.3 9.3 %collective-permute-start.31 = (bf16[112,896]{1,0:T(8,128)(2,1)S(1)}, bf16[112,896]{1,0:T(8,128)(2,1)S(1)}, u32[]{:S(2)}, u32[]{:S(2)}) collective-permute-start(bf16[112,896]{1,0:T(8,128)(2,1)S(1)} %collective-permute-done.30.refs_2_), channel_id=1, source_target_pairs={{0,7},{16,23},{1,0},{17,16},{2,1},{18,17},{3,2},{19,18},{4,3},{20,... | collective-permute-start | bytes 602120 | tf_op jit(solution)/shard_map/ppermute | solution.py:62
  103.8 8.9 %collective-permute-start.25 = (bf16[112,896]{1,0:T(8,128)(2,1)S(1)}, bf16[112,896]{1,0:T(8,128)(2,1)S(1)}, u32[]{:S(2)}, u32[]{:S(2)}) collective-permute-start(bf16[112,896]{1,0:T(8,128)(2,1)S(1)} %collective-permute-done.24.refs_2_), channel_id=1, source_target_pairs={{0,7},{16,23},{1,0},{17,16},{2,1},{18,17},{3,2},{19,18},{4,3},{20,... | collective-permute-start | bytes 602120 | tf_op jit(solution)/shard_map/ppermute | solution.py:62
  108.6 12.8 %collective-permute-start.35 = (bf16[112,896]{1,0:T(8,128)(2,1)S(1)}, bf16[112,896]{1,0:T(8,128)(2,1)S(1)}, u32[]{:S(2)}, u32[]{:S(2)}) collective-permute-start(bf16[112,896]{1,0:T(8,128)(2,1)S(1)} %collective-permute-done.34.refs_6_), channel_id=1, source_target_pairs={{0,1},{16,17},{1,2},{17,18},{2,3},{18,19},{3,4},{19,20},{4,5},{20,... | collective-permute-start | bytes 602120 | tf_op jit(solution)/shard_map/ppermute | solution.py:62
  108.6 12.8 %collective-permute-start.32 = (bf16[112,896]{1,0:T(8,128)(2,1)S(1)}, bf16[112,896]{1,0:T(8,128)(2,1)S(1)}, u32[]{:S(2)}, u32[]{:S(2)}) collective-permute-start(bf16[112,896]{1,0:T(8,128)(2,1)S(1)} %collective-permute-done.31.refs_3_), channel_id=1, source_target_pairs={{0,7},{16,23},{1,0},{17,16},{2,1},{18,17},{3,2},{19,18},{4,3},{20,... | collective-permute-start | bytes 602120 | tf_op jit(solution)/shard_map/ppermute | solution.py:62
  119.6 8.3 %collective-permute-start.28 = (bf16[112,1152]{1,0:T(8,128)(2,1)S(1)}, bf16[112,1152]{1,0:T(8,128)(2,1)S(1)}, u32[]{:S(2)}, u32[]{:S(2)}) collective-permute-start(bf16[112,1152]{1,0:T(8,128)(2,1)S(1)} %shard_map.67), channel_id=1, source_target_pairs={{0,8},{16,24},{1,9},{17,25},{2,10},{18,26},{3,11},{19,27},{4,12},{... | collective-permute-start | bytes 774152 | tf_op jit(solution)/shard_map/ppermute | solution.py:62
  (13 other events, 99.8 us)
Sparse Core Ops, SparseCore 0:
  10.4 48.4 all-gather.4
  61.3 50.2 all-gather.6
